TPU v7x, 1024 devices: a whole 4x8x16 slice. The times are simulated.
1024 devices in a mesh: dp: 128 (over x, y_lo, z), group: 8 (over y_hi, core).
Axes of the slice: x: 4, y: 8 (y_hi: 4, y_lo: 2; y = y_hi * 2 + y_lo), z: 16, core: 2. Of those that a mesh axis runs over, the one named last changes fastest.
Arguments:
- activations: bfloat16 [65536, 2048], P('dp', 'group'), may hold values from -6 to 6
- cotangent: bfloat16 [65536, 704], P('dp'), may hold values from -0.0234375 to 0.0234375
- momentum: float32 [8, 256, 704], P('group', 'dp'), may hold values from -256 to 256, as said below
Outputs:
- update: bfloat16 [8, 256, 704], P('group', 'dp')
- momentum_new: float32 [8, 256, 704], P('group', 'dp')
Inputs may be any that keep to these rules, and one draw needn't show every extreme that they name: The momentum buffer's entries.
All inputs are finite; a program needn't handle non-finite values.
Results may differ from a plain program's by a relative error of at most 0.015.
Values may be sent and summed in bfloat16 or wider, within the bound.
No kernel may reach another device: no remote copies, remote signals or barrier semaphores. Data moves between devices by JAX's collectives and lax.ppermute only.
A program may use at most 32 MiB of HBM per device.

v0:
```python
import jax
import jax.numpy as jnp
from jax import lax
from jax.sharding import PartitionSpec as P

DM = 2048
FE = 704
ITERS = 3


quintic_a = 3.4445
quintic_b = -4.775
quintic_c = 2.0315


def per_device(activations, cotangent, momentum):
    own_rows = momentum.shape[1]
    own_start = lax.axis_index("dp") * own_rows
    gradient = lax.psum_scatter(
        lax.dot_general(
            activations, cotangent, (((0,), (0,)), ((), ())), preferred_element_type=jnp.float32
        ),
        "dp",
        scatter_dimension=0,
        tiled=True,
    )
    momentum_new = 0.95 * momentum[0] + gradient
    direction = gradient + 0.95 * momentum_new
    square_sum = lax.psum(jnp.sum(direction * direction), ("dp", "group"))
    scaled = (direction / (jnp.sqrt(square_sum) + 1e-07)).astype(jnp.bfloat16)
    orthogonal = lax.all_gather(scaled, "dp", axis=0, tiled=True)
    for sweep in range(ITERS):
        current = orthogonal
        gram_piece = lax.psum_scatter(
            lax.dot_general(
                current, current, (((0,), (0,)), ((), ())), preferred_element_type=jnp.float32
            ).astype(jnp.bfloat16),
            "group",
            scatter_dimension=0,
            tiled=True,
        )
        gram_matrix = lax.all_gather(gram_piece, "group", axis=0, tiled=True)
        square = jnp.dot(gram_matrix, gram_matrix, preferred_element_type=jnp.float32)
        polynomial = (quintic_b * gram_matrix.astype(jnp.float32) + quintic_c * square).astype(
            jnp.bfloat16
        )
        product = jnp.dot(current, polynomial, preferred_element_type=jnp.float32)
        orthogonal = (quintic_a * current.astype(jnp.float32) + product).astype(jnp.bfloat16)
    own_block = lax.dynamic_slice_in_dim(orthogonal, own_start, own_rows, 0)
    step_scale = 0.2 * max(DM, FE) ** 0.5
    update = (step_scale * own_block.astype(jnp.float32)).astype(jnp.bfloat16)
    return (update[None], momentum_new[None])


def solution(mesh):
    in_specs = (P("dp", "group"), P("dp", None), P("group", "dp", None))
    out_specs = (P("group", "dp", None), P("group", "dp", None))
    return jax.shard_map(
        per_device, mesh=mesh, in_specs=in_specs, out_specs=out_specs, check_vma=False
    )
```

profile of v0, /device:TPU:1, one launch (start us, length us, event | category | flops | bytes accessed | tf_op | source)
XLA Modules:
  0.0 1789.6 jit_solution(10716831426633686541)
XLA Ops:
  7.2 0.0 copy-start
  7.2 0.0 copy-start.1
  7.2 0.0 all-reduce.3.cloned.1.call-start
  7.2 1.0 copy-done
  8.3 2.3 fusion.15
  10.5 0.0 all-reduce.3.cloned.1.call-update
  10.6 0.0 reduce-scatter.4.cloned.1.call-start
  10.6 1.3 dynamic-slice
  12.6 1084.1 %all-reduce.3.cloned.1.call-done = f32[256,704]{1,0:T(8,128)} async-done(((f32[256,704]{1,0:T(8,128)}), f32[256,704]{1,0:T(8,128)}) %all-reduce.3.cloned.1.call-update) | async-done | bytes 720912
  1096.6 0.0 copy-done.1
  1096.6 1.9 multiply_reduce_fusion
  1098.5 187.7 %psum.7 = f32[]{:T(128)} all-reduce(f32[]{:T(128)} %get-tuple-element.8), channel_id=1, replica_groups=mesh['dp'=128,'group'=8] {'dp','group'}, use_global_device_ids=true, to_apply=%region_2.0 | all-reduce | flops 1 | bytes 8 | tf_op jit(solution)/shard_map/psum | solution.py:29
  1286.9 247.6 %all-gather = bf16[128,2,704]{2,1,0:T(2,128)(2,1)S(1)} all-gather(bf16[1,2,704]{2,1,0:T(2,128)(2,1)S(1)} %fusion.7), channel_id=1, replica_groups=mesh['dp'=128,'group'=8] {'dp'}, dimensions={0}, use_global_device_ids=true | all-gather | bytes 363264 | tf_op jit(solution)/shard_map/all_gather | solution.py:31
  1534.5 0.3 reshape.7
  1534.8 1.5 convolution_convert_fusion.2
  1536.3 0.0 reduce-scatter.4.cloned.1.call-update
  1536.3 0.0 reduce-scatter.6.cloned.1.call-start
  1536.4 0.2 copy.11
  1536.5 90.1 %reduce-scatter.4.cloned.1.call-done = bf16[88,704]{1,0:T(8,128)(2,1)} async-done(((bf16[704,704]{1,0:T(8,128)(2,1)}), bf16[88,704]{1,0:T(8,128)(2,1)}) %reduce-scatter.4.cloned.1.call-update) | async-done | bytes 123920 | tf_op jit(solution)/shard_map/reduce_scatter | solution.py:34
  1626.7 18.6 %all_gather.13 = bf16[704,704]{1,0:T(8,128)(2,1)S(1)} all-gather(bf16[88,704]{1,0:T(8,128)(2,1)} %reduce-scatter.4.cloned.1.call-done), channel_id=1, replica_groups=mesh['dp'=128,'group'=8] {'group'}, dimensions={0}, use_global_device_ids=true | all-gather | bytes 1115136 | tf_op jit(solution)/shard_map/all_gather | solution.py:42
  1645.3 1.8 fusion
  1647.1 1.5 convolution_convert_fusion.1
  1648.5 0.0 reduce-scatter.6.cloned.1.call-update
  1648.6 0.0 reduce-scatter.8.cloned.1.call-start
  1648.6 45.4 %reduce-scatter.6.cloned.1.call-done = bf16[88,704]{1,0:T(8,128)(2,1)} async-done(((bf16[704,704]{1,0:T(8,128)(2,1)}), bf16[88,704]{1,0:T(8,128)(2,1)}) %reduce-scatter.6.cloned.1.call-update) | async-done | bytes 123920 | tf_op jit(solution)/shard_map/reduce_scatter | solution.py:34
  1694.0 18.7 %all_gather.14 = bf16[704,704]{1,0:T(8,128)(2,1)S(1)} all-gather(bf16[88,704]{1,0:T(8,128)(2,1)} %reduce-scatter.6.cloned.1.call-done), channel_id=1, replica_groups=mesh['dp'=128,'group'=8] {'group'}, dimensions={0}, use_global_device_ids=true | all-gather | bytes 1115136 | tf_op jit(solution)/shard_map/all_gather | solution.py:42
  1712.7 1.8 fusion.1
  1714.5 1.5 convolution_convert_fusion
  1715.9 0.0 reduce-scatter.8.cloned.1.call-update
  1716.0 45.2 %reduce-scatter.8.cloned.1.call-done = bf16[88,704]{1,0:T(8,128)(2,1)} async-done(((bf16[704,704]{1,0:T(8,128)(2,1)}), bf16[88,704]{1,0:T(8,128)(2,1)}) %reduce-scatter.8.cloned.1.call-update) | async-done | bytes 123920 | tf_op jit(solution)/shard_map/reduce_scatter | solution.py:34
  1761.2 19.3 %all_gather.15 = bf16[704,704]{1,0:T(8,128)(2,1)S(1)} all-gather(bf16[88,704]{1,0:T(8,128)(2,1)} %reduce-scatter.8.cloned.1.call-done), channel_id=1, replica_groups=mesh['dp'=128,'group'=8] {'group'}, dimensions={0}, use_global_device_ids=true | all-gather | bytes 1115136 | tf_op jit(solution)/shard_map/all_gather | solution.py:42
  1780.4 1.7 fusion.2
  1782.2 0.2 fusion.6
  1782.4 0.7 copy.13
  (1 shorter events, 0.0 us)
Async XLA Ops:
  7.2 1.1 copy-start
  7.2 1089.4 %copy-start.1 = (f32[1,2,704]{2,1,0:T(2,128)S(1)}, f32[1,2,704]{2,1,0:T(2,128)}, u32[]{:S(2)}) copy-start(f32[1,2,704]{2,1,0:T(2,128)} %param.5) | copy-start | bytes 16900
  7.2 1089.4 %all-reduce.3.cloned.1.call-start = ((), (), s32[]{:S(2)}) async-start(), calls=%async_computation.6 | async-start | bytes 1572864
  10.6 1616.1 %reduce-scatter.4.cloned.1.call-start = ((), (), s32[]{:S(2)}) async-start(), calls=%async_computation.3 | async-start | bytes 1216512 | tf_op jit(solution)/shard_map/reduce_scatter | solution.py:34
  1536.3 157.7 %reduce-scatter.6.cloned.1.call-start = ((), (), s32[]{:S(2)}) async-start(), calls=%async_computation.4 | async-start | bytes 1216512 | tf_op jit(solution)/shard_map/reduce_scatter | solution.py:34
  1648.6 112.6 %reduce-scatter.8.cloned.1.call-start = ((), (), s32[]{:S(2)}) async-start(), calls=%async_computation.5 | async-start | bytes 1216512 | tf_op jit(solution)/shard_map/reduce_scatter | solution.py:34
Sparse Core Ops, SparseCore 0:
  11.5 1085.0 all-reduce.2
  1536.4 90.1 reduce-scatter.3
  1648.7 45.2 reduce-scatter.5
  1716.1 45.0 reduce-scatter.7
where the time goes:
time: 1790 us
  waiting for transfers between devices  1260 us (70%)
  blocking collectives  492 us (27%)
    unnamed x5, waiting for transfers between devices  1080 us
    all_gather x1, blocking collectives, per_device(): orthogonal = lax.all_gather(scaled, 'dp', axis=0, tiled=True)  248 us
    psum x1, blocking collectives, per_device(): square_sum = lax.psum(jnp.sum(direction * direction), ('dp', 'group'))  188 us
    reduce_scatter x3, waiting for transfers between devices, per_device(): lax.psum_scatter(lax.dot_general(current, current, (((0,), (0,)), ((), ()...  181 us
    all_gather x3, blocking collectives, per_device(): gram_matrix = lax.all_gather(gram_piece, 'group', axis=0, tiled=True)  56.6 us
  transfers between devices with their start and end apart: 4, of which 4 were waited for; matrix products, arithmetic and copies ran while one was open for 0% of the time, Pallas kernels for 0%

commit v1 on v0

v1 whole, which is shorter than its diff:
```python
import jax
import jax.numpy as jnp
from jax import lax
from jax.experimental import pallas as pl
from jax.experimental.pallas import tpu as pltpu
from jax.sharding import Mesh, PartitionSpec as P

DM = 2048
FE = 704
ITERS = 3
WIDE = 768

quintic_a = 3.4445
quintic_b = -4.775
quintic_c = 2.0315

AXES = ("x", "ylo", "z", "yhi", "core")
SIZES = (4, 2, 16, 4, 2)
NEAR = ("x", "ylo")
FAR = ("z", "yhi")

f32 = jnp.float32
bf16 = jnp.bfloat16


def mm(a, b):
    return jnp.dot(a, b, preferred_element_type=f32)


def newton_schulz_kernel(mine_ref, other_ref, rows_ref, out_ref, gram_ref, poly_ref, left_ref, next_ref):
    total = jnp.zeros((128, 128), f32)
    for t in range(WIDE // 128):
        block = pl.ds(t * 128, 128)
        total += mine_ref[block, block] + other_ref[block, block].astype(f32)
    eye = lax.broadcasted_iota(jnp.int32, (128, 128), 0) == lax.broadcasted_iota(
        jnp.int32, (128, 128), 1
    )
    square_sum = jnp.sum(jnp.where(eye, total, 0.0), keepdims=True)
    scale = 1.0 / (jnp.sqrt(square_sum) + 1e-07)
    gram_ref[...] = ((mine_ref[...] + other_ref[...].astype(f32)) * scale * scale).astype(bf16)
    x = (rows_ref[...] * scale).astype(bf16)

    def right(rows, matrix_ref):
        return mm(rows, matrix_ref[...])

    def polynomial(g_ref):
        square = mm(g_ref[...], g_ref[...])
        poly_ref[...] = (quintic_b * g_ref[...].astype(f32) + quintic_c * square).astype(bf16)

    def step(rows):
        return (quintic_a * rows.astype(f32) + right(rows, poly_ref)).astype(bf16)

    polynomial(gram_ref)
    x = step(x)
    left_ref[...] = (
        quintic_a * gram_ref[...].astype(f32) + mm(poly_ref[...], gram_ref[...])
    ).astype(bf16)
    next_ref[...] = (
        quintic_a * left_ref[...].astype(f32) + mm(left_ref[...], poly_ref[...])
    ).astype(bf16)
    polynomial(next_ref)
    x = step(x)
    left_ref[...] = (
        quintic_a * next_ref[...].astype(f32) + mm(poly_ref[...], next_ref[...])
    ).astype(bf16)
    gram_ref[...] = (
        quintic_a * left_ref[...].astype(f32) + mm(left_ref[...], poly_ref[...])
    ).astype(bf16)
    once = right(x, gram_ref)
    twice = right(once.astype(bf16), gram_ref)
    x = (quintic_a * x.astype(f32) + (quintic_b * once + quintic_c * twice)).astype(bf16)
    step_scale = 0.2 * max(DM, FE) ** 0.5
    out_ref[...] = (step_scale * x.astype(f32)).astype(bf16)


def newton_schulz(mine, other, rows):
    return pl.pallas_call(
        newton_schulz_kernel,
        out_shape=jax.ShapeDtypeStruct((16, WIDE), bf16),
        in_specs=[pl.BlockSpec(memory_space=pltpu.VMEM)] * 3,
        out_specs=pl.BlockSpec(memory_space=pltpu.VMEM),
        scratch_shapes=[pltpu.VMEM((WIDE, WIDE), bf16)] * 4,
        compiler_params=pltpu.CompilerParams(vmem_limit_bytes=48 * 1024 * 1024),
    )(mine, other, rows)


def spread(block, axes, members):
    copies = jnp.broadcast_to(block[None], (members,) + block.shape)
    return lax.all_to_all(copies, axes, 0, 0, tiled=True)


def per_device(activations, cotangent, momentum):
    partial = lax.dot_general(
        activations, cotangent, (((0,), (0,)), ((), ())), preferred_element_type=f32
    ).astype(bf16)
    near = lax.all_to_all(partial.reshape(8, 32, FE), NEAR, 0, 0, tiled=True)
    near = jnp.sum(near.astype(f32), axis=0).astype(bf16)
    far = lax.all_to_all(near.reshape(16, 2, FE), "z", 0, 0, tiled=True)
    gradient = jnp.sum(far.astype(f32), axis=0)
    momentum_new = 0.95 * momentum[0] + gradient
    direction = gradient + 0.95 * momentum_new
    wide = jnp.pad(direction, ((0, 0), (0, WIDE - FE)))
    rows = spread(wide.astype(bf16), FAR, 64).reshape(128, WIDE)
    rows = spread(rows, NEAR, 8).reshape(1024, WIDE)
    mine = lax.dot_general(rows, rows, (((0,), (0,)), ((), ())), preferred_element_type=f32)
    other = lax.ppermute(mine.astype(bf16), "core", [(0, 1), (1, 0)])
    update = newton_schulz(mine, other, jnp.pad(wide, ((0, 14), (0, 0))))
    return (update[None, :2, :FE], momentum_new[None])


def solution(mesh):
    fine = Mesh(mesh.devices.reshape(SIZES), AXES)
    tokens, owners = ("x", "ylo", "z"), ("yhi", "core")
    in_specs = (P(tokens, owners), P(tokens, None), P(owners, tokens, None))
    out_specs = (P(owners, tokens, None), P(owners, tokens, None))
    return jax.shard_map(
        per_device, mesh=fine, in_specs=in_specs, out_specs=out_specs, check_vma=False
    )
```

time: 1790 us -> 112 us (0.06)
  waiting for transfers between devices: 1260 us -> 1.82 us
  blocking collectives: 492 us -> 88.5 us
    unnamed x5 -> x0, waiting for transfers between devices: 1080 us -> none
    all_gather x4 -> x0, blocking collectives: 304 us -> none  [the longest x1 248 us: per_device(): orthogonal = lax.all_gather(scaled, 'dp', axis=0, tiled=True)]
    psum x1 -> x0, blocking collectives: 188 us -> none  [per_device(): square_sum = lax.psum(jnp.sum(direction * direction), ('dp', 'group'))]
    reduce_scatter x3 -> x0, waiting for transfers between devices: 181 us -> none  [per_device(): lax.psum_scatter(lax.dot_general(current, current, (((0,), (0,)), ((), ()...]
    all_to_all x0 -> x4, blocking collectives: none -> 88.5 us  [the longest x2 45.1 us: spread(): return lax.all_to_all(copies, axes, 0, 0, tiled=True)]
  transfers between devices with their start and end apart: 4 -> 1, of which waited for: 4 -> 1; matrix products, arithmetic and copies ran while one was open for 0% -> 1% of each run, Pallas kernels for 0% -> 0%
where the time goes in v1:
time: 112 us
  blocking collectives  88.5 us (79%)
  starting transfers between devices  8.03 us (7%)
  Pallas kernels  7.37 us (7%)
  matrix products  2.75 us (2%)
  local copies, waits for them, and re-layouts  2.21 us (2%)
  waiting for transfers between devices  1.82 us (2%)
    all_to_all x2, blocking collectives, spread(): return lax.all_to_all(copies, axes, 0, 0, tiled=True)  45.1 us
    all_to_all x1, blocking collectives, per_device(): far = lax.all_to_all(near.reshape(16, 2, FE), 'z', 0, 0, tiled=True)  30.8 us
    all_to_all x1, blocking collectives, per_device(): near = lax.all_to_all(partial.reshape(8, 32, FE), NEAR, 0, 0, tiled=True)  12.6 us
    ppermute x1, starting transfers between devices, per_device(): other = lax.ppermute(mine.astype(bf16), 'core', [(0, 1), (1, 0)])  8.03 us
    pallas_call x1, Pallas kernels, newton_schulz(): pl.pallas_call(newton_schulz_kernel, out_shape=jax.ShapeDtypeStruct((16,...  7.37 us
  transfers between devices with their start and end apart: 1, of which 1 were waited for; matrix products, arithmetic and copies ran while one was open for 1% of the time, Pallas kernels for 0%

profile of v1, /device:TPU:1, one launch (start us, length us, event | category | flops | bytes accessed | tf_op | source)
XLA Modules:
  0.0 112.1 jit_solution(4411246895102580639)
XLA Ops:
  0.6 0.0 copy-start
  0.6 1.1 copy-done
  1.7 0.0 copy-start.1
  1.7 1.3 %convolution_convert_fusion = bf16[256,704]{0,1:T(8,128)(2,1)S(1)} fusion(bf16[512,704]{0,1:T(8,128)(2,1)S(1)} %copy-done, bf16[512,256]{1,0:T(8,128)(2,1)} %param.3), kind=kOutput, calls=%fused_computation.1 | convolution fusion | flops 184729600 | bytes 1343488 | tf_op jit(solution)/shard_map/dot_general | solution.py:93
  3.1 0.2 copy.16
  3.2 12.6 %all_to_all.20 = bf16[8,32,704]{2,1,0:T(8,128)(2,1)S(1)} all-to-all(bf16[8,32,704]{2,1,0:T(8,128)(2,1)S(1)} %bitcast.17), channel_id=1, replica_groups=mesh['x'=4,'ylo'=2,'z'=16,'yhi'=4,'core'=2] {'x','ylo'}, dimensions={0} | all-to-all | bytes 720896 | tf_op jit(solution)/shard_map/all_to_all | solution.py:96
  15.8 0.1 reduce_sum.23
  15.9 30.8 %all_to_all.21 = bf16[16,2,704]{2,1,0:T(2,128)(2,1)S(1)} all-to-all(bf16[16,2,704]{2,1,0:T(2,128)(2,1)S(1)} %reshape.17), channel_id=1, replica_groups=mesh['x'=4,'ylo'=2,'z'=16,'yhi'=4,'core'=2] {'z'}, dimensions={0} | all-to-all | bytes 90112 | tf_op jit(solution)/shard_map/all_to_all | solution.py:98
  46.8 0.0 copy-done.1
  46.9 0.1 broadcast_in_dim.8
  47.0 26.4 %all_to_all.22 = bf16[64,2,768]{2,1,0:T(2,128)(2,1)S(1)} all-to-all(bf16[64,2,768]{2,1,0:T(2,128)(2,1)S(1)} %broadcast_in_dim.8), channel_id=1, replica_groups=mesh['x'=4,'ylo'=2,'z'=16,'yhi'=4,'core'=2] {'z','yhi'}, dimensions={0} | all-to-all | bytes 393216 | tf_op jit(solution)/shard_map/all_to_all | solution.py:89
  73.4 0.1 broadcast_in_dim.18
  73.5 0.1 broadcast_in_dim.19
  73.6 18.7 %all_to_all.23 = bf16[8,128,768]{2,1,0:T(8,128)(2,1)S(1)} all-to-all(bf16[8,128,768]{2,1,0:T(8,128)(2,1)S(1)} %broadcast_in_dim.19), channel_id=1, replica_groups=mesh['x'=4,'ylo'=2,'z'=16,'yhi'=4,'core'=2] {'x','ylo'}, dimensions={0} | all-to-all | bytes 3145728 | tf_op jit(solution)/shard_map/all_to_all | solution.py:89
  92.2 1.4 %fusion.2 = (bf16[768,768]{1,0:T(8,128)(2,1)S(1)}, f32[768,768]{1,0:T(8,128)S(1)}) fusion(bf16[8,128,768]{2,1,0:T(8,128)(2,1)S(1)} %all_to_all.23), kind=kOutput, calls=%fused_computation.9 | convolution fusion | flops 1208549376 | bytes 5111808 | tf_op jit(solution)/shard_map/dot_general | solution.py:105
  93.7 8.0 %collective-permute-start = (bf16[768,768]{1,0:T(8,128)(2,1)S(1)}, bf16[768,768]{1,0:T(8,128)(2,1)S(1)}, u32[]{:S(2)}, u32[]{:S(2)}) collective-permute-start(bf16[768,768]{1,0:T(8,128)(2,1)S(1)} %get-tuple-element.2), channel_id=1, source_target_pairs={{0,1},{1,0},{2,3},{3,2},{4,5},{5,4},{6,7},{7,6},{8,9},{9,8},{10,11... | collective-permute-start | bytes 3538952 | tf_op jit(solution)/shard_map/ppermute | solution.py:106
  101.8 0.6 bitcast_add_fusion
  102.4 1.8 %collective-permute-done.other_ref = bf16[768,768]{1,0:T(8,128)(2,1)S(1)} collective-permute-done((bf16[768,768]{1,0:T(8,128)(2,1)S(1)}, bf16[768,768]{1,0:T(8,128)(2,1)S(1)}, u32[]{:S(2)}, u32[]{:S(2)}) %collective-permute-start) | collective-permute-done | bytes 1179680 | tf_op jit(solution)/shard_map/ppermute | solution.py:106
  104.2 7.4 %shard_map.50 = bf16[16,768]{1,0:T(8,128)(2,1)S(1)} custom-call(f32[768,768]{1,0:T(8,128)S(1)} %get-tuple-element.3.mine_ref, bf16[768,768]{1,0:T(8,128)(2,1)S(1)} %collective-permute-done.other_ref, f32[16,768]{1,0:T(8,128)S(1)} %pad.9.rows_ref), custom_call_target="tpu_custom_call" | custom-call | tf_op jit(solution)/shard_map/pallas_call | solution.py:77
  111.6 0.6 slice_bitcast_fusion
  (6 shorter events, 0.1 us)
Async XLA Ops:
  0.6 1.1 copy-start
  1.7 45.1 %copy-start.1 = (f32[1,2,704]{2,1,0:T(2,128)S(1)}, f32[1,2,704]{2,1,0:T(2,128)}, u32[]{:S(2)}) copy-start(f32[1,2,704]{2,1,0:T(2,128)} %param.5) | copy-start | bytes 16900
  93.7 10.5 %collective-permute-start = (bf16[768,768]{1,0:T(8,128)(2,1)S(1)}, bf16[768,768]{1,0:T(8,128)(2,1)S(1)}, u32[]{:S(2)}, u32[]{:S(2)}) collective-permute-start(bf16[768,768]{1,0:T(8,128)(2,1)S(1)} %get-tuple-element.2), channel_id=1, source_target_pairs={{0,1},{1,0},{2,3},{3,2},{4,5},{5,4},{6,7},{7,6},{8,9},{9,8},{10,11... | collective-permute-start | bytes 3538952 | tf_op jit(solution)/shard_map/ppermute | solution.py:106

commit v2 on v1

v2 whole, which is shorter than its diff:
```python
import jax
import jax.numpy as jnp
from jax import lax
from jax.experimental import pallas as pl
from jax.experimental.pallas import tpu as pltpu
from jax.sharding import Mesh, PartitionSpec as P

DM = 2048
FE = 704
ITERS = 3
WIDE = 768
SHARE = 256
TILE = 256
BLOCK = 16

quintic_a = 3.4445
quintic_b = -4.775
quintic_c = 2.0315
step_scale = 0.2 * max(DM, FE) ** 0.5

AXES = ("x", "ylo", "zhi", "zlo", "yhi", "core")
SIZES = (4, 2, 8, 2, 4, 2)
NEAR = ("x", "ylo", "zlo")
FAR = "zhi"
OWNERS = "yhi"

f32 = jnp.float32
bf16 = jnp.bfloat16


def mm(a, b):
    return jnp.dot(a, b, preferred_element_type=f32)


def mm_nt(a, b):
    return lax.dot_general(a, b, (((1,), (1,)), ((), ())), preferred_element_type=f32)


def kernel_call(kernel, out_shape, n_in, scratch=(), mib=32):
    return pl.pallas_call(
        kernel,
        out_shape=out_shape,
        in_specs=[pl.BlockSpec(memory_space=pltpu.VMEM)] * n_in,
        out_specs=jax.tree.map(lambda _: pl.BlockSpec(memory_space=pltpu.VMEM), out_shape),
        scratch_shapes=list(scratch),
        compiler_params=pltpu.CompilerParams(vmem_limit_bytes=mib * 1024 * 1024),
    )


def gradient_kernel(act_ref, cot_ref, out_ref):
    to = lax.broadcasted_iota(jnp.int32, (SHARE, SHARE), 0)
    source = lax.broadcasted_iota(jnp.int32, (SHARE, SHARE), 1)
    wanted = (to & ~31) + ((to & 15) >> 1) * 4 + ((to & 31) >> 4) * 2 + (to & 1)
    order = jnp.where(wanted == source, 1.0, 0.0).astype(bf16)
    left = mm_nt(order, act_ref[...]).astype(bf16)
    out_ref[:, :FE] = mm_nt(left, cot_ref[...]).astype(bf16)
    out_ref[:, FE:] = jnp.zeros((SHARE, WIDE - FE), bf16)


def own_rows_mask():
    row = lax.broadcasted_iota(jnp.int32, (BLOCK, WIDE), 0)
    return (row >> 1) == lax.axis_index(FAR)


def place_rows(mom_ref):
    row = lax.broadcasted_iota(jnp.int32, (BLOCK, FE), 0)
    first = jnp.broadcast_to(mom_ref[0:1, :], (BLOCK, FE))
    second = jnp.broadcast_to(mom_ref[1:2, :], (BLOCK, FE))
    rows = jnp.where((row & 1) == 0, first, second)
    return jnp.concatenate([rows, jnp.zeros((BLOCK, WIDE - FE), f32)], axis=1)


def share_kernel(near_ref, mom_ref, exact_ref, out_ref):
    partial = jnp.sum(near_ref[...].astype(f32), axis=0)
    own = jnp.where(own_rows_mask(), place_rows(mom_ref), 0.0)
    share = 1.95 * partial + (0.95 * 0.95) * own
    exact_ref[...] = share
    out_ref[...] = jnp.broadcast_to(share.astype(bf16)[None], out_ref.shape)


def direction_kernel(far_ref, exact_ref, mom_ref, rows_ref, own_ref, new_ref):
    total = jnp.sum(far_ref[...].astype(f32), axis=0)
    rows_ref[...] = jnp.broadcast_to(total.astype(bf16)[None], rows_ref.shape)
    exact = exact_ref[...]
    better = total + (exact - exact.astype(bf16).astype(f32))
    mine = jnp.where(own_rows_mask(), better, 0.0)
    odd = (lax.broadcasted_iota(jnp.int32, (BLOCK, WIDE), 0) & 1) == 1
    first = jnp.sum(jnp.where(odd, 0.0, mine), axis=0, keepdims=True)
    second = jnp.sum(jnp.where(odd, mine, 0.0), axis=0, keepdims=True)
    own_ref[...] = jnp.zeros_like(own_ref)
    own_ref[0:1, :] = first
    own_ref[1:2, :] = second
    for r, direction in enumerate((first, second)):
        old = mom_ref[r : r + 1, :]
        gradient = (direction[:, :FE] - (0.95 * 0.95) * old) / 1.95
        new_ref[r : r + 1, :] = 0.95 * old + gradient


def newton_schulz_kernel(
    mine_ref, other_ref, rows_ref, out_ref, gram_ref, poly_ref, left_ref, next_ref
):
    total = jnp.zeros((128, 128), f32)
    for t in range(WIDE // 128):
        block = pl.ds(t * 128, 128)
        total += mine_ref[block, block] + other_ref[block, block].astype(f32)
    eye = lax.broadcasted_iota(jnp.int32, (128, 128), 0) == lax.broadcasted_iota(
        jnp.int32, (128, 128), 1
    )
    square_sum = jnp.sum(jnp.where(eye, total, 0.0), keepdims=True)
    scale = 1.0 / (jnp.sqrt(square_sum) + 1e-07)
    gram_ref[...] = ((mine_ref[...] + other_ref[...].astype(f32)) * scale * scale).astype(bf16)
    x = (rows_ref[...] * scale).astype(bf16)

    def symmetric(to_ref, a_ref, b_ref, finish):
        for i in range(WIDE // TILE):
            rows, cols = pl.ds(i * TILE, TILE), pl.ds(i * TILE, WIDE - i * TILE)
            value = finish(rows, cols, mm(a_ref[rows, :], b_ref[:, cols])).astype(bf16)
            to_ref[rows, cols] = value
            for j in range(i + 1, WIDE // TILE):
                at = (j - i) * TILE
                to_ref[pl.ds(j * TILE, TILE), rows] = value[:, at : at + TILE].T

    def polynomial(g_ref):
        def finish(rows, cols, square):
            return quintic_b * g_ref[rows, cols].astype(f32) + quintic_c * square

        symmetric(poly_ref, g_ref, g_ref, finish)

    def one_side(to_ref, a_ref, b_ref, base_ref):
        def finish(rows, cols, product):
            return quintic_a * base_ref[rows, cols].astype(f32) + product

        symmetric(to_ref, a_ref, b_ref, finish)

    def step(rows):
        return quintic_a * rows.astype(f32) + mm(rows, poly_ref[...])

    polynomial(gram_ref)
    x = step(x).astype(bf16)
    one_side(left_ref, poly_ref, gram_ref, gram_ref)
    one_side(next_ref, left_ref, poly_ref, left_ref)
    polynomial(next_ref)
    x = step(x).astype(bf16)

    def last_gram(rows):
        rows = step(rows).astype(bf16)
        return step(mm(rows, next_ref[...]).astype(bf16))

    once = last_gram(x)
    twice = last_gram(once.astype(bf16))
    x = (quintic_a * x.astype(f32) + (quintic_b * once + quintic_c * twice)).astype(bf16)
    out_ref[...] = (step_scale * x.astype(f32)).astype(bf16)[:2, :FE]


def shape(dims, dtype):
    return jax.ShapeDtypeStruct(dims, dtype)


def exchange(blocks, axes):
    return lax.all_to_all(blocks, axes, 0, 0, tiled=True)


def per_device(activations, cotangent, momentum):
    momentum = momentum[0]
    partial = kernel_call(gradient_kernel, shape((SHARE, WIDE), bf16), 2)(activations, cotangent.T)
    near = exchange(partial.reshape(16, BLOCK, WIDE), NEAR)
    exact, share = kernel_call(
        share_kernel, (shape((BLOCK, WIDE), f32), shape((8, BLOCK, WIDE), bf16)), 2
    )(near, momentum)
    far = exchange(share, FAR)
    rows, own, momentum_new = kernel_call(
        direction_kernel,
        (shape((4, BLOCK, WIDE), bf16), shape((16, WIDE), f32), shape((2, FE), f32)),
        3,
    )(far, exact, momentum)
    rows = exchange(rows, OWNERS).reshape(64, WIDE)
    rows = exchange(jnp.broadcast_to(rows[None], (16, 64, WIDE)), NEAR).reshape(1024, WIDE)
    mine = lax.dot_general(rows, rows, (((0,), (0,)), ((), ())), preferred_element_type=f32)
    other = lax.ppermute(mine.astype(bf16), "core", [(0, 1), (1, 0)])
    update = kernel_call(
        newton_schulz_kernel, shape((2, FE), bf16), 3, [pltpu.VMEM((WIDE, WIDE), bf16)] * 4, 48
    )(mine, other, own)
    return (update[None], momentum_new[None])


def solution(mesh):
    fine = Mesh(mesh.devices.reshape(SIZES), AXES)
    tokens, owners = ("x", "ylo", "zhi", "zlo"), ("yhi", "core")
    in_specs = (P(tokens, owners), P(tokens, None), P(owners, tokens, None))
    out_specs = (P(owners, tokens, None), P(owners, tokens, None))
    return jax.shard_map(
        per_device, mesh=fine, in_specs=in_specs, out_specs=out_specs, check_vma=False
    )
```

time: 112 us -> 101 us (0.902)
  blocking collectives: 88.5 us -> 76.3 us
  starting transfers between devices: 8.03 us -> 11 us
  matrix products: 2.75 us -> 1.45 us
    all_to_all x4, blocking collectives: 88.5 us -> 76.3 us  [exchange(): return lax.all_to_all(blocks, axes, 0, 0, tiled=True)]
    ppermute x1, starting transfers between devices: 8.03 us -> 11 us  [per_device(): other = lax.ppermute(mine.astype(bf16), 'core', [(0, 1), (1, 0)])]
    dot_general x1 -> x0, matrix products: 1.31 us -> none  [per_device(): lax.dot_general(activations, cotangent, (((0,), (0,)), ((), ())), preferr...]
    pallas_call x1 -> x4, Pallas kernels: 7.37 us -> 6.58 us  [the longest x1 5.27 us: per_device(): kernel_call(newton_schulz_kernel, shape((2, FE), bf16), 3, [pltpu.VMEM((W...]
  transfers between devices with their start and end apart: 1 -> 1, of which waited for: 1 -> 1; matrix products, arithmetic and copies ran while one was open for 1% -> 0% of each run, Pallas kernels for 0% -> 0%
where the time goes in v2:
time: 101 us
  blocking collectives  76.3 us (76%)
  starting transfers between devices  11 us (11%)
  Pallas kernels  6.58 us (7%)
  waiting for transfers between devices  2.45 us (2%)
  local copies, waits for them, and re-layouts  2.2 us (2%)
  matrix products  1.45 us (1%)
    all_to_all x4, blocking collectives, exchange(): return lax.all_to_all(blocks, axes, 0, 0, tiled=True)  76.3 us
    ppermute x1, starting transfers between devices, per_device(): other = lax.ppermute(mine.astype(bf16), 'core', [(0, 1), (1, 0)])  11 us
    pallas_call x1, Pallas kernels, per_device(): kernel_call(newton_schulz_kernel, shape((2, FE), bf16), 3, [pltpu.VMEM((W...  5.27 us
    ppermute x1, waiting for transfers between devices, per_device(): other = lax.ppermute(mine.astype(bf16), 'core', [(0, 1), (1, 0)])  2.45 us
    unnamed x6, local copies, waits for them, and re-layouts  2.06 us
  transfers between devices with their start and end apart: 1, of which 1 were waited for; matrix products, arithmetic and copies ran while one was open for 0% of the time, Pallas kernels for 0%

profile of v2, /device:TPU:1, one launch (start us, length us, event | category | flops | bytes accessed | tf_op | source)
XLA Modules:
  0.0 100.6 jit_solution(650364273390926609)
XLA Ops:
  0.6 0.0 copy-start
  0.6 1.1 %copy-done = bf16[512,704]{0,1:T(8,128)(2,1)S(1)} copy-done((bf16[512,704]{0,1:T(8,128)(2,1)S(1)}, bf16[512,704]{0,1:T(8,128)(2,1)}, u32[]{:S(2)}) %copy-start) | copy-done | bytes 720920
  1.7 0.0 copy-start.1
  1.7 0.9 copy-done.1
  2.7 0.0 copy-start.2
  2.7 0.6 shard_map.50
  3.3 14.3 %all_to_all.20.near_ref = bf16[16,16,768]{2,1,0:T(8,128)(2,1)S(1)} all-to-all(bf16[16,16,768]{2,1,0:T(8,128)(2,1)S(1)} %bitcast.10), channel_id=1, replica_groups=mesh['x'=4,'ylo'=2,'zhi'=8,'zlo'=2,'yhi'=4,'core'=2] {'x','ylo','zlo'}, dimensions={0} | all-to-all | bytes 786432 | tf_op jit(solution)/shard_map/all_to_all | solution.py:160
  17.6 0.0 copy-done.2
  17.6 0.1 shard_map.51
  17.7 32.1 %all_to_all.21.far_ref = bf16[8,16,768]{2,1,0:T(8,128)(2,1)S(1)} all-to-all(bf16[8,16,768]{2,1,0:T(8,128)(2,1)S(1)} %get-tuple-element.7), channel_id=1, replica_groups=mesh['x'=4,'ylo'=2,'zhi'=8,'zlo'=2,'yhi'=4,'core'=2] {'zhi'}, dimensions={0} | all-to-all | bytes 393216 | tf_op jit(solution)/shard_map/all_to_all | solution.py:160
  49.8 0.7 shard_map.52
  50.5 12.8 %all_to_all.22 = bf16[4,16,768]{2,1,0:T(8,128)(2,1)S(1)} all-to-all(bf16[4,16,768]{2,1,0:T(8,128)(2,1)S(1)} %get-tuple-element.9), channel_id=1, replica_groups=mesh['x'=4,'ylo'=2,'zhi'=8,'zlo'=2,'yhi'=4,'core'=2] {'yhi'}, dimensions={0} | all-to-all | bytes 196608 | tf_op jit(solution)/shard_map/all_to_all | solution.py:160
  63.3 0.1 broadcast_in_dim.14
  63.4 17.1 %all_to_all.23 = bf16[16,64,768]{2,1,0:T(8,128)(2,1)S(1)} all-to-all(bf16[16,64,768]{2,1,0:T(8,128)(2,1)S(1)} %broadcast_in_dim.14), channel_id=1, replica_groups=mesh['x'=4,'ylo'=2,'zhi'=8,'zlo'=2,'yhi'=4,'core'=2] {'x','ylo','zlo'}, dimensions={0} | all-to-all | bytes 3145728 | tf_op jit(solution)/shard_map/all_to_all | solution.py:160
  80.5 1.5 %fusion = (bf16[768,768]{1,0:T(8,128)(2,1)S(1)}, f32[768,768]{1,0:T(8,128)S(1)}) fusion(bf16[16,64,768]{2,1,0:T(8,128)(2,1)S(1)} %all_to_all.23), kind=kOutput, calls=%fused_computation.1 | convolution fusion | flops 1208549376 | bytes 5111808 | tf_op jit(solution)/shard_map/dot_general | solution.py:178
  81.9 11.0 %collective-permute-start = (bf16[768,768]{1,0:T(8,128)(2,1)S(1)}, bf16[768,768]{1,0:T(8,128)(2,1)S(1)}, u32[]{:S(2)}, u32[]{:S(2)}) collective-permute-start(bf16[768,768]{1,0:T(8,128)(2,1)S(1)} %get-tuple-element.12), channel_id=1, source_target_pairs={{0,1},{1,0},{2,3},{3,2},{4,5},{5,4},{6,7},{7,6},{8,9},{9,8},{10,11... | collective-permute-start | bytes 3538952 | tf_op jit(solution)/shard_map/ppermute | solution.py:179
  92.9 2.5 %collective-permute-done.other_ref = bf16[768,768]{1,0:T(8,128)(2,1)S(1)} collective-permute-done((bf16[768,768]{1,0:T(8,128)(2,1)S(1)}, bf16[768,768]{1,0:T(8,128)(2,1)S(1)}, u32[]{:S(2)}, u32[]{:S(2)}) %collective-permute-start) | collective-permute-done | bytes 1179680 | tf_op jit(solution)/shard_map/ppermute | solution.py:179
  95.4 5.3 %shard_map.53 = bf16[2,704]{1,0:T(2,128)(2,1)} custom-call(f32[768,768]{1,0:T(8,128)S(1)} %get-tuple-element.13.mine_ref, bf16[768,768]{1,0:T(8,128)(2,1)S(1)} %collective-permute-done.other_ref, f32[16,768]{1,0:T(8,128)S(1)} %get-tuple-element.10.rows_ref), custom_call_target="tpu_custom_call" | custom-call | tf_op jit(solution)/shard_map/pallas_call | solution.py:180
Async XLA Ops:
  0.6 1.1 %copy-start = (bf16[512,704]{0,1:T(8,128)(2,1)S(1)}, bf16[512,704]{0,1:T(8,128)(2,1)}, u32[]{:S(2)}) copy-start(bf16[512,704]{0,1:T(8,128)(2,1)} %param.4) | copy-start | bytes 2162692
  1.7 0.9 copy-start.1
  2.7 14.9 %copy-start.2 = (f32[1,2,704]{2,1,0:T(2,128)S(1)}, f32[1,2,704]{2,1,0:T(2,128)}, u32[]{:S(2)}) copy-start(f32[1,2,704]{2,1,0:T(2,128)} %param.5) | copy-start | bytes 16900
  81.9 13.4 %collective-permute-start = (bf16[768,768]{1,0:T(8,128)(2,1)S(1)}, bf16[768,768]{1,0:T(8,128)(2,1)S(1)}, u32[]{:S(2)}, u32[]{:S(2)}) collective-permute-start(bf16[768,768]{1,0:T(8,128)(2,1)S(1)} %get-tuple-element.12), channel_id=1, source_target_pairs={{0,1},{1,0},{2,3},{3,2},{4,5},{5,4},{6,7},{7,6},{8,9},{9,8},{10,11... | collective-permute-start | bytes 3538952 | tf_op jit(solution)/shard_map/ppermute | solution.py:179

commit v3 on v2

--- a/solution.py
+++ b/solution.py
@@ -36,25 +36,37 @@
     return lax.dot_general(a, b, (((1,), (1,)), ((), ())), preferred_element_type=f32)
 
 
-def kernel_call(kernel, out_shape, n_in, scratch=(), mib=32):
+def kernel_call(kernel, out_shape, n_in, scratch=(), mib=32, space=pltpu.VMEM):
     return pl.pallas_call(
         kernel,
         out_shape=out_shape,
-        in_specs=[pl.BlockSpec(memory_space=pltpu.VMEM)] * n_in,
+        in_specs=[pl.BlockSpec(memory_space=space)] * n_in,
         out_specs=jax.tree.map(lambda _: pl.BlockSpec(memory_space=pltpu.VMEM), out_shape),
         scratch_shapes=list(scratch),
         compiler_params=pltpu.CompilerParams(vmem_limit_bytes=mib * 1024 * 1024),
     )
 
 
-def gradient_kernel(act_ref, cot_ref, out_ref):
+def gradient_kernel(act_hbm, cot_hbm, out_ref, act_ref, cot_ref, act_sem, cot_sems):
+    fetch_act = pltpu.make_async_copy(act_hbm, act_ref, act_sem)
+    fetch_act.start()
+    fetches = []
+    for j, at in enumerate(range(0, FE, TILE)):
+        part = pl.ds(at, min(TILE, FE - at))
+        fetches.append(
+            (part, pltpu.make_async_copy(cot_hbm.at[part], cot_ref.at[part], cot_sems.at[j]))
+        )
+        fetches[-1][1].start()
     to = lax.broadcasted_iota(jnp.int32, (SHARE, SHARE), 0)
     source = lax.broadcasted_iota(jnp.int32, (SHARE, SHARE), 1)
     wanted = (to & ~31) + ((to & 15) >> 1) * 4 + ((to & 31) >> 4) * 2 + (to & 1)
     order = jnp.where(wanted == source, 1.0, 0.0).astype(bf16)
+    out_ref[:, FE:] = jnp.zeros((SHARE, WIDE - FE), bf16)
+    fetch_act.wait()
     left = mm_nt(order, act_ref[...]).astype(bf16)
-    out_ref[:, :FE] = mm_nt(left, cot_ref[...]).astype(bf16)
-    out_ref[:, FE:] = jnp.zeros((SHARE, WIDE - FE), bf16)
+    for part, fetch in fetches:
+        fetch.wait()
+        out_ref[:, part] = mm_nt(left, cot_ref[part, :]).astype(bf16)
 
 
 def own_rows_mask():
@@ -78,47 +90,67 @@
     out_ref[...] = jnp.broadcast_to(share.astype(bf16)[None], out_ref.shape)
 
 
-def direction_kernel(far_ref, exact_ref, mom_ref, rows_ref, own_ref, new_ref):
+def direction_kernel(far_ref, exact_ref, rows_ref, own_ref):
     total = jnp.sum(far_ref[...].astype(f32), axis=0)
     rows_ref[...] = jnp.broadcast_to(total.astype(bf16)[None], rows_ref.shape)
     exact = exact_ref[...]
     better = total + (exact - exact.astype(bf16).astype(f32))
     mine = jnp.where(own_rows_mask(), better, 0.0)
     odd = (lax.broadcasted_iota(jnp.int32, (BLOCK, WIDE), 0) & 1) == 1
-    first = jnp.sum(jnp.where(odd, 0.0, mine), axis=0, keepdims=True)
-    second = jnp.sum(jnp.where(odd, mine, 0.0), axis=0, keepdims=True)
     own_ref[...] = jnp.zeros_like(own_ref)
-    own_ref[0:1, :] = first
-    own_ref[1:2, :] = second
-    for r, direction in enumerate((first, second)):
-        old = mom_ref[r : r + 1, :]
-        gradient = (direction[:, :FE] - (0.95 * 0.95) * old) / 1.95
-        new_ref[r : r + 1, :] = 0.95 * old + gradient
+    own_ref[0:1, :] = jnp.sum(jnp.where(odd, 0.0, mine), axis=0, keepdims=True)
+    own_ref[1:2, :] = jnp.sum(jnp.where(odd, mine, 0.0), axis=0, keepdims=True)
+
+
+def packed_blocks():
+    at = 0
+    for first in range(0, WIDE, TILE):
+        yield first, at, WIDE - first
+        at += WIDE - first
+
+
+def gram_kernel(rows_ref, out_ref):
+    for first, at, width in packed_blocks():
+        out_ref[:, at : at + width] = lax.dot_general(
+            rows_ref[:, first : first + TILE],
+            rows_ref[:, first:],
+            (((0,), (0,)), ((), ())),
+            preferred_element_type=f32,
+        ).astype(bf16)
 
 
 def newton_schulz_kernel(
     mine_ref, other_ref, rows_ref, out_ref, gram_ref, poly_ref, left_ref, next_ref
 ):
     total = jnp.zeros((128, 128), f32)
-    for t in range(WIDE // 128):
-        block = pl.ds(t * 128, 128)
-        total += mine_ref[block, block] + other_ref[block, block].astype(f32)
+    for _, at, _ in packed_blocks():
+        for half in range(0, TILE, 128):
+            rows, cols = pl.ds(half, 128), pl.ds(at + half, 128)
+            total += mine_ref[rows, cols].astype(f32) + other_ref[rows, cols].astype(f32)
     eye = lax.broadcasted_iota(jnp.int32, (128, 128), 0) == lax.broadcasted_iota(
         jnp.int32, (128, 128), 1
     )
     square_sum = jnp.sum(jnp.where(eye, total, 0.0), keepdims=True)
     scale = 1.0 / (jnp.sqrt(square_sum) + 1e-07)
-    gram_ref[...] = ((mine_ref[...] + other_ref[...].astype(f32)) * scale * scale).astype(bf16)
     x = (rows_ref[...] * scale).astype(bf16)
 
+    def store_symmetric(to_ref, first, value):
+        rows = pl.ds(first, TILE)
+        to_ref[rows, pl.ds(first, WIDE - first)] = value
+        for later in range(first + TILE, WIDE, TILE):
+            at = later - first
+            to_ref[pl.ds(later, TILE), rows] = value[:, at : at + TILE].T
+
+    for first, at, width in packed_blocks():
+        cols = pl.ds(at, width)
+        both = mine_ref[:, cols].astype(f32) + other_ref[:, cols].astype(f32)
+        store_symmetric(gram_ref, first, (both * scale * scale).astype(bf16))
+
     def symmetric(to_ref, a_ref, b_ref, finish):
-        for i in range(WIDE // TILE):
-            rows, cols = pl.ds(i * TILE, TILE), pl.ds(i * TILE, WIDE - i * TILE)
+        for first in range(0, WIDE, TILE):
+            rows, cols = pl.ds(first, TILE), pl.ds(first, WIDE - first)
             value = finish(rows, cols, mm(a_ref[rows, :], b_ref[:, cols])).astype(bf16)
-            to_ref[rows, cols] = value
-            for j in range(i + 1, WIDE // TILE):
-                at = (j - i) * TILE
-                to_ref[pl.ds(j * TILE, TILE), rows] = value[:, at : at + TILE].T
+            store_symmetric(to_ref, first, value)
 
     def polynomial(g_ref):
         def finish(rows, cols, square):
@@ -162,23 +194,35 @@
 
 def per_device(activations, cotangent, momentum):
     momentum = momentum[0]
-    partial = kernel_call(gradient_kernel, shape((SHARE, WIDE), bf16), 2)(activations, cotangent.T)
+    partial = kernel_call(
+        gradient_kernel,
+        shape((SHARE, WIDE), bf16),
+        2,
+        [
+            pltpu.VMEM((512, SHARE), bf16),
+            pltpu.VMEM((FE, 512), bf16),
+            pltpu.SemaphoreType.DMA,
+            pltpu.SemaphoreType.DMA((3,)),
+        ],
+        mib=60,
+        space=pltpu.HBM,
+    )(activations, cotangent.T)
     near = exchange(partial.reshape(16, BLOCK, WIDE), NEAR)
     exact, share = kernel_call(
         share_kernel, (shape((BLOCK, WIDE), f32), shape((8, BLOCK, WIDE), bf16)), 2
     )(near, momentum)
     far = exchange(share, FAR)
-    rows, own, momentum_new = kernel_call(
-        direction_kernel,
-        (shape((4, BLOCK, WIDE), bf16), shape((16, WIDE), f32), shape((2, FE), f32)),
-        3,
-    )(far, exact, momentum)
+    rows, own = kernel_call(
+        direction_kernel, (shape((4, BLOCK, WIDE), bf16), shape((16, WIDE), f32)), 2
+    )(far, exact)
     rows = exchange(rows, OWNERS).reshape(64, WIDE)
     rows = exchange(jnp.broadcast_to(rows[None], (16, 64, WIDE)), NEAR).reshape(1024, WIDE)
-    mine = lax.dot_general(rows, rows, (((0,), (0,)), ((), ())), preferred_element_type=f32)
-    other = lax.ppermute(mine.astype(bf16), "core", [(0, 1), (1, 0)])
+    mine = kernel_call(gram_kernel, shape((TILE, 1536), bf16), 1)(rows)
+    other = lax.ppermute(mine, "core", [(0, 1), (1, 0)])
+    gradient = (own[:2, :FE] - (0.95 * 0.95) * momentum) / 1.95
+    momentum_new = 0.95 * momentum + gradient
     update = kernel_call(
-        newton_schulz_kernel, shape((2, FE), bf16), 3, [pltpu.VMEM((WIDE, WIDE), bf16)] * 4, 48
+        newton_schulz_kernel, shape((2, FE), bf16), 3, [pltpu.VMEM((WIDE, WIDE), bf16)] * 4, mib=48
     )(mine, other, own)
     return (update[None], momentum_new[None])
 

time: 101 us -> 100 us (0.990)
  Pallas kernels: 6.58 us -> 9.55 us
  local copies, waits for them, and re-layouts: 2.2 us -> 0.15 us
  matrix products: 1.45 us -> 0 us
  waiting for transfers between devices: 2.45 us -> 1.29 us
    pallas_call x1 -> x2, Pallas kernels: 0.57 us -> 4.16 us  [the longest x1 3.15 us: per_device(): kernel_call(gradient_kernel, shape((SHARE, WIDE), bf16), 2, [pltpu.VMEM((...]
    unnamed x6 -> x2, local copies, waits for them, and re-layouts: 2.06 us -> 0.01 us
    dot_general x1 -> x0, matrix products: 1.45 us -> none  [per_device(): lax.dot_general(rows, rows, (((0,), (0,)), ((), ())), preferred_element_t...]
    ppermute x1, waiting for transfers between devices: 2.45 us -> 1.29 us  [per_device(): other = lax.ppermute(mine, 'core', [(0, 1), (1, 0)])]
  transfers between devices with their start and end apart: 1 -> 1, of which waited for: 1 -> 1; matrix products, arithmetic and copies ran while one was open for 0% -> 1% of each run, Pallas kernels for 0% -> 0%
where the time goes in v3:
time: 100 us; the launch traced here: 99.8 us
  blocking collectives  76.5 us (76%)
  starting transfers between devices  11 us (11%)
  Pallas kernels  9.55 us (10%)
  waiting for transfers between devices  1.29 us (1%)
    all_to_all x4, blocking collectives, exchange(): return lax.all_to_all(blocks, axes, 0, 0, tiled=True)  76.5 us
    ppermute x1, starting transfers between devices, per_device(): other = lax.ppermute(mine, 'core', [(0, 1), (1, 0)])  11 us
    pallas_call x1, Pallas kernels, per_device(): kernel_call(newton_schulz_kernel, shape((2, FE), bf16), 3, [pltpu.VMEM((W...  5.26 us
    pallas_call x1, Pallas kernels, per_device(): kernel_call(gradient_kernel, shape((SHARE, WIDE), bf16), 2, [pltpu.VMEM((...  3.15 us
  transfers between devices with their start and end apart: 1, of which 1 were waited for; matrix products, arithmetic and copies ran while one was open for 1% of the time, Pallas kernels for 0%

profile of v3, /device:TPU:1, one launch (start us, length us, event | category | flops | bytes accessed | tf_op | source)
XLA Modules:
  0.0 99.8 jit_solution(4012663185639032663)
XLA Ops:
  0.6 0.0 copy-start
  0.6 3.2 %shard_map.50 = bf16[256,768]{1,0:T(8,128)(2,1)} custom-call(bf16[512,256]{1,0:T(8,128)(2,1)} %act_hbm.1, bf16[704,512]{1,0:T(8,128)(2,1)} %bitcast.12), custom_call_target="tpu_custom_call" | custom-call | tf_op jit(solution)/shard_map/pallas_call | solution.py:197
  3.8 14.6 %all_to_all.20.near_ref = bf16[16,16,768]{2,1,0:T(8,128)(2,1)S(1)} all-to-all(bf16[16,16,768]{2,1,0:T(8,128)(2,1)} %bitcast.11), channel_id=1, replica_groups=mesh['x'=4,'ylo'=2,'zhi'=8,'zlo'=2,'yhi'=4,'core'=2] {'x','ylo','zlo'}, dimensions={0} | all-to-all | bytes 786432 | tf_op jit(solution)/shard_map/all_to_all | solution.py:192
  18.4 0.0 copy-done
  18.4 0.1 shard_map.51
  18.4 32.1 %all_to_all.21.far_ref = bf16[8,16,768]{2,1,0:T(8,128)(2,1)S(1)} all-to-all(bf16[8,16,768]{2,1,0:T(8,128)(2,1)S(1)} %get-tuple-element.6), channel_id=1, replica_groups=mesh['x'=4,'ylo'=2,'zhi'=8,'zlo'=2,'yhi'=4,'core'=2] {'zhi'}, dimensions={0} | all-to-all | bytes 393216 | tf_op jit(solution)/shard_map/all_to_all | solution.py:192
  50.6 0.1 shard_map.52
  50.6 12.8 %all_to_all.22 = bf16[4,16,768]{2,1,0:T(8,128)(2,1)S(1)} all-to-all(bf16[4,16,768]{2,1,0:T(8,128)(2,1)S(1)} %get-tuple-element.8), channel_id=1, replica_groups=mesh['x'=4,'ylo'=2,'zhi'=8,'zlo'=2,'yhi'=4,'core'=2] {'yhi'}, dimensions={0} | all-to-all | bytes 196608 | tf_op jit(solution)/shard_map/all_to_all | solution.py:192
  63.4 0.1 broadcast_in_dim.14
  63.6 17.1 %all_to_all.23 = bf16[16,64,768]{2,1,0:T(8,128)(2,1)S(1)} all-to-all(bf16[16,64,768]{2,1,0:T(8,128)(2,1)S(1)} %broadcast_in_dim.14), channel_id=1, replica_groups=mesh['x'=4,'ylo'=2,'zhi'=8,'zlo'=2,'yhi'=4,'core'=2] {'x','ylo','zlo'}, dimensions={0} | all-to-all | bytes 3145728 | tf_op jit(solution)/shard_map/all_to_all | solution.py:192
  80.6 1.0 %shard_map.53.mine_ref = bf16[256,1536]{1,0:T(8,128)(2,1)S(1)} custom-call(bf16[1024,768]{1,0:T(8,128)(2,1)S(1)} %bitcast.9), custom_call_target="tpu_custom_call" | custom-call | tf_op jit(solution)/shard_map/pallas_call | solution.py:220
  81.6 11.0 %collective-permute-start = (bf16[256,1536]{1,0:T(8,128)(2,1)S(1)}, bf16[256,1536]{1,0:T(8,128)(2,1)S(1)}, u32[]{:S(2)}, u32[]{:S(2)}) collective-permute-start(bf16[256,1536]{1,0:T(8,128)(2,1)S(1)} %shard_map.53.mine_ref), channel_id=1, source_target_pairs={{0,1},{1,0},{2,3},{3,2},{4,5},{5,4},{6,7},{7,6},{8,9},{9,8},{10,11... | collective-permute-start | bytes 2359304 | tf_op jit(solution)/shard_map/ppermute | solution.py:221
  92.6 0.6 add_bitcast_fusion
  93.2 1.3 %collective-permute-done.other_ref = bf16[256,1536]{1,0:T(8,128)(2,1)S(1)} collective-permute-done((bf16[256,1536]{1,0:T(8,128)(2,1)S(1)}, bf16[256,1536]{1,0:T(8,128)(2,1)S(1)}, u32[]{:S(2)}, u32[]{:S(2)}) %collective-permute-start) | collective-permute-done | bytes 786464 | tf_op jit(solution)/shard_map/ppermute | solution.py:221
  94.5 5.3 %shard_map.54 = bf16[2,704]{1,0:T(2,128)(2,1)} custom-call(bf16[256,1536]{1,0:T(8,128)(2,1)S(1)} %shard_map.53.mine_ref, bf16[256,1536]{1,0:T(8,128)(2,1)S(1)} %collective-permute-done.other_ref, f32[16,768]{1,0:T(8,128)S(1)} %get-tuple-element.9.rows_ref), custom_call_target="tpu_custom_call" | custom-call | tf_op jit(solution)/shard_map/pallas_call | solution.py:224
Async XLA Ops:
  0.6 17.7 %copy-start = (f32[1,2,704]{2,1,0:T(2,128)S(1)}, f32[1,2,704]{2,1,0:T(2,128)}, u32[]{:S(2)}) copy-start(f32[1,2,704]{2,1,0:T(2,128)} %param.5) | copy-start | bytes 16900
  81.6 12.9 %collective-permute-start = (bf16[256,1536]{1,0:T(8,128)(2,1)S(1)}, bf16[256,1536]{1,0:T(8,128)(2,1)S(1)}, u32[]{:S(2)}, u32[]{:S(2)}) collective-permute-start(bf16[256,1536]{1,0:T(8,128)(2,1)S(1)} %shard_map.53.mine_ref), channel_id=1, source_target_pairs={{0,1},{1,0},{2,3},{3,2},{4,5},{5,4},{6,7},{7,6},{8,9},{9,8},{10,11... | collective-permute-start | bytes 2359304 | tf_op jit(solution)/shard_map/ppermute | solution.py:221

commit v4 on v3

--- a/solution.py
+++ b/solution.py
@@ -36,37 +36,25 @@
     return lax.dot_general(a, b, (((1,), (1,)), ((), ())), preferred_element_type=f32)
 
 
-def kernel_call(kernel, out_shape, n_in, scratch=(), mib=32, space=pltpu.VMEM):
+def kernel_call(kernel, out_shape, n_in, scratch=(), mib=32):
     return pl.pallas_call(
         kernel,
         out_shape=out_shape,
-        in_specs=[pl.BlockSpec(memory_space=space)] * n_in,
+        in_specs=[pl.BlockSpec(memory_space=pltpu.VMEM)] * n_in,
         out_specs=jax.tree.map(lambda _: pl.BlockSpec(memory_space=pltpu.VMEM), out_shape),
         scratch_shapes=list(scratch),
         compiler_params=pltpu.CompilerParams(vmem_limit_bytes=mib * 1024 * 1024),
     )
 
 
-def gradient_kernel(act_hbm, cot_hbm, out_ref, act_ref, cot_ref, act_sem, cot_sems):
-    fetch_act = pltpu.make_async_copy(act_hbm, act_ref, act_sem)
-    fetch_act.start()
-    fetches = []
-    for j, at in enumerate(range(0, FE, TILE)):
-        part = pl.ds(at, min(TILE, FE - at))
-        fetches.append(
-            (part, pltpu.make_async_copy(cot_hbm.at[part], cot_ref.at[part], cot_sems.at[j]))
-        )
-        fetches[-1][1].start()
+def gradient_kernel(act_ref, cot_ref, out_ref):
     to = lax.broadcasted_iota(jnp.int32, (SHARE, SHARE), 0)
     source = lax.broadcasted_iota(jnp.int32, (SHARE, SHARE), 1)
     wanted = (to & ~31) + ((to & 15) >> 1) * 4 + ((to & 31) >> 4) * 2 + (to & 1)
     order = jnp.where(wanted == source, 1.0, 0.0).astype(bf16)
+    left = mm_nt(order, act_ref[...]).astype(bf16)
+    out_ref[:, :FE] = mm_nt(left, cot_ref[...]).astype(bf16)
     out_ref[:, FE:] = jnp.zeros((SHARE, WIDE - FE), bf16)
-    fetch_act.wait()
-    left = mm_nt(order, act_ref[...]).astype(bf16)
-    for part, fetch in fetches:
-        fetch.wait()
-        out_ref[:, part] = mm_nt(left, cot_ref[part, :]).astype(bf16)
 
 
 def own_rows_mask():
@@ -194,19 +182,7 @@
 
 def per_device(activations, cotangent, momentum):
     momentum = momentum[0]
-    partial = kernel_call(
-        gradient_kernel,
-        shape((SHARE, WIDE), bf16),
-        2,
-        [
-            pltpu.VMEM((512, SHARE), bf16),
-            pltpu.VMEM((FE, 512), bf16),
-            pltpu.SemaphoreType.DMA,
-            pltpu.SemaphoreType.DMA((3,)),
-        ],
-        mib=60,
-        space=pltpu.HBM,
-    )(activations, cotangent.T)
+    partial = kernel_call(gradient_kernel, shape((SHARE, WIDE), bf16), 2)(activations, cotangent.T)
     near = exchange(partial.reshape(16, BLOCK, WIDE), NEAR)
     exact, share = kernel_call(
         share_kernel, (shape((BLOCK, WIDE), f32), shape((8, BLOCK, WIDE), bf16)), 2

time: 100 us -> 99.4 us (level)
  Pallas kernels: 9.55 us -> 6.97 us
  local copies, waits for them, and re-layouts: 0.15 us -> 2.2 us
    pallas_call x1, Pallas kernels: 3.15 us -> 0.57 us  [per_device(): kernel_call(gradient_kernel, shape((SHARE, WIDE), bf16), 2)]
    unnamed x2 -> x6, local copies, waits for them, and re-layouts: 0.01 us -> 2.06 us
where the time goes in v4:
time: 99.4 us; the launch traced here: 99 us
  blocking collectives  76.3 us (77%)
  starting transfers between devices  11 us (11%)
  Pallas kernels  6.97 us (7%)
  local copies, waits for them, and re-layouts  2.2 us (2%)
  waiting for transfers between devices  1.29 us (1%)
    all_to_all x4, blocking collectives, exchange(): return lax.all_to_all(blocks, axes, 0, 0, tiled=True)  76.3 us
    ppermute x1, starting transfers between devices, per_device(): other = lax.ppermute(mine, 'core', [(0, 1), (1, 0)])  11 us
    pallas_call x1, Pallas kernels, per_device(): kernel_call(newton_schulz_kernel, shape((2, FE), bf16), 3, [pltpu.VMEM((W...  5.26 us
    unnamed x6, local copies, waits for them, and re-layouts  2.06 us
  transfers between devices with their start and end apart: 1, of which 1 were waited for; matrix products, arithmetic and copies ran while one was open for 1% of the time, Pallas kernels for 0%

profile of v4, /device:TPU:1, one launch (start us, length us, event | category | flops | bytes accessed | tf_op | source)
XLA Modules:
  0.0 99.0 jit_solution(5534441410891986855)
XLA Ops:
  0.6 0.0 copy-start
  0.6 1.1 %copy-done = bf16[512,704]{0,1:T(8,128)(2,1)S(1)} copy-done((bf16[512,704]{0,1:T(8,128)(2,1)S(1)}, bf16[512,704]{0,1:T(8,128)(2,1)}, u32[]{:S(2)}) %copy-start) | copy-done | bytes 720920
  1.7 0.0 copy-start.1
  1.7 0.9 copy-done.1
  2.7 0.0 copy-start.2
  2.7 0.6 shard_map.50
  3.3 14.3 %all_to_all.20.near_ref = bf16[16,16,768]{2,1,0:T(8,128)(2,1)S(1)} all-to-all(bf16[16,16,768]{2,1,0:T(8,128)(2,1)S(1)} %bitcast.10), channel_id=1, replica_groups=mesh['x'=4,'ylo'=2,'zhi'=8,'zlo'=2,'yhi'=4,'core'=2] {'x','ylo','zlo'}, dimensions={0} | all-to-all | bytes 786432 | tf_op jit(solution)/shard_map/all_to_all | solution.py:180
  17.6 0.0 copy-done.2
  17.6 0.1 shard_map.51
  17.7 32.1 %all_to_all.21.far_ref = bf16[8,16,768]{2,1,0:T(8,128)(2,1)S(1)} all-to-all(bf16[8,16,768]{2,1,0:T(8,128)(2,1)S(1)} %get-tuple-element.6), channel_id=1, replica_groups=mesh['x'=4,'ylo'=2,'zhi'=8,'zlo'=2,'yhi'=4,'core'=2] {'zhi'}, dimensions={0} | all-to-all | bytes 393216 | tf_op jit(solution)/shard_map/all_to_all | solution.py:180
  49.8 0.1 shard_map.52
  49.9 12.8 %all_to_all.22 = bf16[4,16,768]{2,1,0:T(8,128)(2,1)S(1)} all-to-all(bf16[4,16,768]{2,1,0:T(8,128)(2,1)S(1)} %get-tuple-element.8), channel_id=1, replica_groups=mesh['x'=4,'ylo'=2,'zhi'=8,'zlo'=2,'yhi'=4,'core'=2] {'yhi'}, dimensions={0} | all-to-all | bytes 196608 | tf_op jit(solution)/shard_map/all_to_all | solution.py:180
  62.7 0.1 broadcast_in_dim.14
  62.8 17.1 %all_to_all.23 = bf16[16,64,768]{2,1,0:T(8,128)(2,1)S(1)} all-to-all(bf16[16,64,768]{2,1,0:T(8,128)(2,1)S(1)} %broadcast_in_dim.14), channel_id=1, replica_groups=mesh['x'=4,'ylo'=2,'zhi'=8,'zlo'=2,'yhi'=4,'core'=2] {'x','ylo','zlo'}, dimensions={0} | all-to-all | bytes 3145728 | tf_op jit(solution)/shard_map/all_to_all | solution.py:180
  79.9 1.0 %shard_map.53.mine_ref = bf16[256,1536]{1,0:T(8,128)(2,1)S(1)} custom-call(bf16[1024,768]{1,0:T(8,128)(2,1)S(1)} %bitcast.9), custom_call_target="tpu_custom_call" | custom-call | tf_op jit(solution)/shard_map/pallas_call | solution.py:196
  80.9 11.0 %collective-permute-start = (bf16[256,1536]{1,0:T(8,128)(2,1)S(1)}, bf16[256,1536]{1,0:T(8,128)(2,1)S(1)}, u32[]{:S(2)}, u32[]{:S(2)}) collective-permute-start(bf16[256,1536]{1,0:T(8,128)(2,1)S(1)} %shard_map.53.mine_ref), channel_id=1, source_target_pairs={{0,1},{1,0},{2,3},{3,2},{4,5},{5,4},{6,7},{7,6},{8,9},{9,8},{10,11... | collective-permute-start | bytes 2359304 | tf_op jit(solution)/shard_map/ppermute | solution.py:197
  91.9 0.6 add_bitcast_fusion
  92.5 1.3 %collective-permute-done.other_ref = bf16[256,1536]{1,0:T(8,128)(2,1)S(1)} collective-permute-done((bf16[256,1536]{1,0:T(8,128)(2,1)S(1)}, bf16[256,1536]{1,0:T(8,128)(2,1)S(1)}, u32[]{:S(2)}, u32[]{:S(2)}) %collective-permute-start) | collective-permute-done | bytes 786464 | tf_op jit(solution)/shard_map/ppermute | solution.py:197
  93.8 5.3 %shard_map.54 = bf16[2,704]{1,0:T(2,128)(2,1)} custom-call(bf16[256,1536]{1,0:T(8,128)(2,1)S(1)} %shard_map.53.mine_ref, bf16[256,1536]{1,0:T(8,128)(2,1)S(1)} %collective-permute-done.other_ref, f32[16,768]{1,0:T(8,128)S(1)} %get-tuple-element.9.rows_ref), custom_call_target="tpu_custom_call" | custom-call | tf_op jit(solution)/shard_map/pallas_call | solution.py:200
Async XLA Ops:
  0.6 1.1 %copy-start = (bf16[512,704]{0,1:T(8,128)(2,1)S(1)}, bf16[512,704]{0,1:T(8,128)(2,1)}, u32[]{:S(2)}) copy-start(bf16[512,704]{0,1:T(8,128)(2,1)} %param.4) | copy-start | bytes 2162692
  1.7 0.9 copy-start.1
  2.7 14.9 %copy-start.2 = (f32[1,2,704]{2,1,0:T(2,128)S(1)}, f32[1,2,704]{2,1,0:T(2,128)}, u32[]{:S(2)}) copy-start(f32[1,2,704]{2,1,0:T(2,128)} %param.5) | copy-start | bytes 16900
  80.9 12.9 %collective-permute-start = (bf16[256,1536]{1,0:T(8,128)(2,1)S(1)}, bf16[256,1536]{1,0:T(8,128)(2,1)S(1)}, u32[]{:S(2)}, u32[]{:S(2)}) collective-permute-start(bf16[256,1536]{1,0:T(8,128)(2,1)S(1)} %shard_map.53.mine_ref), channel_id=1, source_target_pairs={{0,1},{1,0},{2,3},{3,2},{4,5},{5,4},{6,7},{7,6},{8,9},{9,8},{10,11... | collective-permute-start | bytes 2359304 | tf_op jit(solution)/shard_map/ppermute | solution.py:197

commit v5 on v4

--- a/solution.py
+++ b/solution.py
@@ -25,6 +25,7 @@
 OWNERS = "yhi"
 
 f32 = jnp.float32
+COST = pl.CostEstimate(flops=4_000_000_000, bytes_accessed=1_000_000, transcendentals=0)
 bf16 = jnp.bfloat16
 
 
@@ -36,24 +37,28 @@
     return lax.dot_general(a, b, (((1,), (1,)), ((), ())), preferred_element_type=f32)
 
 
-def kernel_call(kernel, out_shape, n_in, scratch=(), mib=32):
+def kernel_call(kernel, out_shape, n_in, scratch=(), mib=32, cost=None):
     return pl.pallas_call(
         kernel,
         out_shape=out_shape,
         in_specs=[pl.BlockSpec(memory_space=pltpu.VMEM)] * n_in,
         out_specs=jax.tree.map(lambda _: pl.BlockSpec(memory_space=pltpu.VMEM), out_shape),
         scratch_shapes=list(scratch),
+        cost_estimate=cost,
         compiler_params=pltpu.CompilerParams(vmem_limit_bytes=mib * 1024 * 1024),
     )
 
 
-def gradient_kernel(act_ref, cot_ref, out_ref):
+def order_kernel(act_ref, out_ref):
     to = lax.broadcasted_iota(jnp.int32, (SHARE, SHARE), 0)
     source = lax.broadcasted_iota(jnp.int32, (SHARE, SHARE), 1)
     wanted = (to & ~31) + ((to & 15) >> 1) * 4 + ((to & 31) >> 4) * 2 + (to & 1)
     order = jnp.where(wanted == source, 1.0, 0.0).astype(bf16)
-    left = mm_nt(order, act_ref[...]).astype(bf16)
-    out_ref[:, :FE] = mm_nt(left, cot_ref[...]).astype(bf16)
+    out_ref[...] = mm_nt(order, act_ref[...]).astype(bf16)
+
+
+def gradient_kernel(left_ref, cot_ref, out_ref):
+    out_ref[:, :FE] = mm_nt(left_ref[...], cot_ref[...]).astype(bf16)
     out_ref[:, FE:] = jnp.zeros((SHARE, WIDE - FE), bf16)
 
 
@@ -97,7 +102,34 @@
         at += WIDE - first
 
 
-def gram_kernel(rows_ref, out_ref):
+HALF = 32
+ROWS = 64
+PACKED = 352
+TAIL = 640
+
+
+def pack_kernel(rows_ref, out_ref):
+    for at in range(0, TAIL, 128):
+        tile = rows_ref[:, at : at + 128]
+        out_ref[:, at // 2 : at // 2 + ROWS, :] = jnp.broadcast_to(tile[None], (16, ROWS, 128))
+    upper = rows_ref[:HALF, TAIL:].astype(f32)
+    lower = pltpu.roll(rows_ref[HALF:, TAIL:].astype(f32), 64, 1)
+    lane = lax.broadcasted_iota(jnp.int32, (HALF, 128), 1)
+    tile = jnp.where(lane < 64, upper, lower).astype(bf16)
+    out_ref[:, TAIL // 2 :, :] = jnp.broadcast_to(tile[None], (16, HALF, 128))
+
+
+def gram_kernel(packed_ref, out_ref, rows_ref):
+    lane = lax.broadcasted_iota(jnp.int32, (HALF, 128), 1)
+    for m in range(16):
+        first = m * ROWS
+        for at in range(0, TAIL, 128):
+            rows_ref[first : first + ROWS, at : at + 128] = packed_ref[m, at // 2 : at // 2 + ROWS, :]
+        tile = packed_ref[m, TAIL // 2 :, :].astype(f32)
+        upper = jnp.where(lane < 64, tile, 0.0).astype(bf16)
+        lower = jnp.where(lane < 64, pltpu.roll(tile, 64, 1), 0.0).astype(bf16)
+        rows_ref[first : first + HALF, TAIL:] = upper
+        rows_ref[first + HALF : first + ROWS, TAIL:] = lower
     for first, at, width in packed_blocks():
         out_ref[:, at : at + width] = lax.dot_general(
             rows_ref[:, first : first + TILE],
@@ -182,7 +214,8 @@
 
 def per_device(activations, cotangent, momentum):
     momentum = momentum[0]
-    partial = kernel_call(gradient_kernel, shape((SHARE, WIDE), bf16), 2)(activations, cotangent.T)
+    left = kernel_call(order_kernel, shape((SHARE, 512), bf16), 1, cost=COST)(activations)
+    partial = kernel_call(gradient_kernel, shape((SHARE, WIDE), bf16), 2)(left, cotangent.T)
     near = exchange(partial.reshape(16, BLOCK, WIDE), NEAR)
     exact, share = kernel_call(
         share_kernel, (shape((BLOCK, WIDE), f32), shape((8, BLOCK, WIDE), bf16)), 2
@@ -191,9 +224,11 @@
     rows, own = kernel_call(
         direction_kernel, (shape((4, BLOCK, WIDE), bf16), shape((16, WIDE), f32)), 2
     )(far, exact)
-    rows = exchange(rows, OWNERS).reshape(64, WIDE)
-    rows = exchange(jnp.broadcast_to(rows[None], (16, 64, WIDE)), NEAR).reshape(1024, WIDE)
-    mine = kernel_call(gram_kernel, shape((TILE, 1536), bf16), 1)(rows)
+    rows = exchange(rows, OWNERS).reshape(ROWS, WIDE)
+    rows = exchange(kernel_call(pack_kernel, shape((16, PACKED, 128), bf16), 1)(rows), NEAR)
+    mine = kernel_call(
+        gram_kernel, shape((TILE, 1536), bf16), 1, [pltpu.VMEM((1024, WIDE), bf16)]
+    )(rows)
     other = lax.ppermute(mine, "core", [(0, 1), (1, 0)])
     gradient = (own[:2, :FE] - (0.95 * 0.95) * momentum) / 1.95
     momentum_new = 0.95 * momentum + gradient

time: 99.4 us -> 97.5 us (0.981)
  local copies, waits for them, and re-layouts: 2.2 us -> 1.02 us
    unnamed x6, local copies, waits for them, and re-layouts: 2.06 us -> 1.02 us
where the time goes in v5:
time: 97.5 us; the launch traced here: 97.2 us
  blocking collectives  76 us (78%)
  starting transfers between devices  10.3 us (11%)
  Pallas kernels  7.37 us (8%)
  waiting for transfers between devices  1.29 us (1%)
  local copies, waits for them, and re-layouts  1.02 us (1%)
    all_to_all x4, blocking collectives, exchange(): return lax.all_to_all(blocks, axes, 0, 0, tiled=True)  76 us
    ppermute x1, starting transfers between devices, per_device(): other = lax.ppermute(mine, 'core', [(0, 1), (1, 0)])  10.3 us
    pallas_call x1, Pallas kernels, per_device(): kernel_call(newton_schulz_kernel, shape((2, FE), bf16), 3, [pltpu.VMEM((W...  5.26 us
  transfers between devices with their start and end apart: 1, of which 1 were waited for; matrix products, arithmetic and copies ran while one was open for 1% of the time, Pallas kernels for 0%

profile of v5, /device:TPU:1, one launch (start us, length us, event | category | flops | bytes accessed | tf_op | source)
XLA Modules:
  0.0 97.2 jit_solution(13902363185981283908)
XLA Ops:
  0.6 0.0 copy-start
  0.6 0.0 copy-start.2
  0.6 1.0 %copy-done.2 = bf16[512,256]{1,0:T(8,128)(2,1)S(1)} copy-done((bf16[512,256]{1,0:T(8,128)(2,1)S(1)}, bf16[512,256]{1,0:T(8,128)(2,1)}, u32[]{:S(2)}) %copy-start.2) | copy-done | bytes 262168
  1.7 0.3 shard_map.50.left_ref
  1.9 0.0 copy-start.1
  1.9 0.0 copy-done
  2.0 0.4 shard_map.51
  2.4 14.3 %all_to_all.20.near_ref = bf16[16,16,768]{2,1,0:T(8,128)(2,1)S(1)} all-to-all(bf16[16,16,768]{2,1,0:T(8,128)(2,1)S(1)} %bitcast.8), channel_id=1, replica_groups=mesh['x'=4,'ylo'=2,'zhi'=8,'zlo'=2,'yhi'=4,'core'=2] {'x','ylo','zlo'}, dimensions={0} | all-to-all | bytes 786432 | tf_op jit(solution)/shard_map/all_to_all | solution.py:212
  16.7 0.0 copy-done.1
  16.7 0.1 shard_map.52
  16.8 32.1 %all_to_all.21.far_ref = bf16[8,16,768]{2,1,0:T(8,128)(2,1)S(1)} all-to-all(bf16[8,16,768]{2,1,0:T(8,128)(2,1)S(1)} %get-tuple-element.6), channel_id=1, replica_groups=mesh['x'=4,'ylo'=2,'zhi'=8,'zlo'=2,'yhi'=4,'core'=2] {'zhi'}, dimensions={0} | all-to-all | bytes 393216 | tf_op jit(solution)/shard_map/all_to_all | solution.py:212
  48.9 0.1 shard_map.53
  49.0 12.8 %all_to_all.22 = bf16[4,16,768]{2,1,0:T(8,128)(2,1)S(1)} all-to-all(bf16[4,16,768]{2,1,0:T(8,128)(2,1)S(1)} %get-tuple-element.8), channel_id=1, replica_groups=mesh['x'=4,'ylo'=2,'zhi'=8,'zlo'=2,'yhi'=4,'core'=2] {'yhi'}, dimensions={0} | all-to-all | bytes 196608 | tf_op jit(solution)/shard_map/all_to_all | solution.py:212
  61.8 0.2 shard_map.54
  62.0 16.7 %all_to_all.23.packed_ref = bf16[16,352,128]{2,1,0:T(8,128)(2,1)S(1)} all-to-all(bf16[16,352,128]{2,1,0:T(8,128)(2,1)S(1)} %shard_map.54), channel_id=1, replica_groups=mesh['x'=4,'ylo'=2,'zhi'=8,'zlo'=2,'yhi'=4,'core'=2] {'x','ylo','zlo'}, dimensions={0} | all-to-all | bytes 2883584 | tf_op jit(solution)/shard_map/all_to_all | solution.py:212
  78.7 1.1 %shard_map.55.mine_ref = bf16[256,1536]{1,0:T(8,128)(2,1)S(1)} custom-call(bf16[16,352,128]{2,1,0:T(8,128)(2,1)S(1)} %all_to_all.23.packed_ref), custom_call_target="tpu_custom_call" | custom-call | tf_op jit(solution)/shard_map/pallas_call | solution.py:229
  79.8 10.3 %collective-permute-start = (bf16[256,1536]{1,0:T(8,128)(2,1)S(1)}, bf16[256,1536]{1,0:T(8,128)(2,1)S(1)}, u32[]{:S(2)}, u32[]{:S(2)}) collective-permute-start(bf16[256,1536]{1,0:T(8,128)(2,1)S(1)} %shard_map.55.mine_ref), channel_id=1, source_target_pairs={{0,1},{1,0},{2,3},{3,2},{4,5},{5,4},{6,7},{7,6},{8,9},{9,8},{10,11... | collective-permute-start | bytes 2359304 | tf_op jit(solution)/shard_map/ppermute | solution.py:232
  90.1 0.6 add_bitcast_fusion
  90.7 1.3 %collective-permute-done.other_ref = bf16[256,1536]{1,0:T(8,128)(2,1)S(1)} collective-permute-done((bf16[256,1536]{1,0:T(8,128)(2,1)S(1)}, bf16[256,1536]{1,0:T(8,128)(2,1)S(1)}, u32[]{:S(2)}, u32[]{:S(2)}) %collective-permute-start) | collective-permute-done | bytes 786464 | tf_op jit(solution)/shard_map/ppermute | solution.py:232
  92.0 5.3 %shard_map.56 = bf16[2,704]{1,0:T(2,128)(2,1)} custom-call(bf16[256,1536]{1,0:T(8,128)(2,1)S(1)} %shard_map.55.mine_ref, bf16[256,1536]{1,0:T(8,128)(2,1)S(1)} %collective-permute-done.other_ref, f32[16,768]{1,0:T(8,128)S(1)} %get-tuple-element.9.rows_ref), custom_call_target="tpu_custom_call" | custom-call | tf_op jit(solution)/shard_map/pallas_call | solution.py:235
Async XLA Ops:
  0.6 1.3 %copy-start = (bf16[512,704]{0,1:T(8,128)(2,1)S(1)}, bf16[512,704]{0,1:T(8,128)(2,1)}, u32[]{:S(2)}) copy-start(bf16[512,704]{0,1:T(8,128)(2,1)} %param.4) | copy-start | bytes 2162692
  0.6 1.0 %copy-start.2 = (bf16[512,256]{1,0:T(8,128)(2,1)S(1)}, bf16[512,256]{1,0:T(8,128)(2,1)}, u32[]{:S(2)}) copy-start(bf16[512,256]{1,0:T(8,128)(2,1)} %act_ref.1) | copy-start | bytes 786436
  1.9 14.8 %copy-start.1 = (f32[1,2,704]{2,1,0:T(2,128)S(1)}, f32[1,2,704]{2,1,0:T(2,128)}, u32[]{:S(2)}) copy-start(f32[1,2,704]{2,1,0:T(2,128)} %param.5) | copy-start | bytes 16900
  79.8 12.2 %collective-permute-start = (bf16[256,1536]{1,0:T(8,128)(2,1)S(1)}, bf16[256,1536]{1,0:T(8,128)(2,1)S(1)}, u32[]{:S(2)}, u32[]{:S(2)}) collective-permute-start(bf16[256,1536]{1,0:T(8,128)(2,1)S(1)} %shard_map.55.mine_ref), channel_id=1, source_target_pairs={{0,1},{1,0},{2,3},{3,2},{4,5},{5,4},{6,7},{7,6},{8,9},{9,8},{10,11... | collective-permute-start | bytes 2359304 | tf_op jit(solution)/shard_map/ppermute | solution.py:232

commit v6 on v4

--- a/solution.py
+++ b/solution.py
@@ -11,6 +11,8 @@
 WIDE = 768
 SHARE = 256
 TILE = 256
+LINES = 88
+TAIL = 640
 BLOCK = 16
 
 quintic_a = 3.4445
@@ -25,6 +27,7 @@
 OWNERS = "yhi"
 
 f32 = jnp.float32
+COST = pl.CostEstimate(flops=4_000_000_000, bytes_accessed=1_000_000, transcendentals=0)
 bf16 = jnp.bfloat16
 
 
@@ -36,25 +39,52 @@
     return lax.dot_general(a, b, (((1,), (1,)), ((), ())), preferred_element_type=f32)
 
 
-def kernel_call(kernel, out_shape, n_in, scratch=(), mib=32):
+def kernel_call(kernel, out_shape, n_in, scratch=(), mib=32, cost=None):
     return pl.pallas_call(
         kernel,
         out_shape=out_shape,
         in_specs=[pl.BlockSpec(memory_space=pltpu.VMEM)] * n_in,
         out_specs=jax.tree.map(lambda _: pl.BlockSpec(memory_space=pltpu.VMEM), out_shape),
         scratch_shapes=list(scratch),
+        cost_estimate=cost,
         compiler_params=pltpu.CompilerParams(vmem_limit_bytes=mib * 1024 * 1024),
     )
 
 
-def gradient_kernel(act_ref, cot_ref, out_ref):
+def order_kernel(act_ref, out_ref):
     to = lax.broadcasted_iota(jnp.int32, (SHARE, SHARE), 0)
     source = lax.broadcasted_iota(jnp.int32, (SHARE, SHARE), 1)
     wanted = (to & ~31) + ((to & 15) >> 1) * 4 + ((to & 31) >> 4) * 2 + (to & 1)
     order = jnp.where(wanted == source, 1.0, 0.0).astype(bf16)
-    left = mm_nt(order, act_ref[...]).astype(bf16)
-    out_ref[:, :FE] = mm_nt(left, cot_ref[...]).astype(bf16)
-    out_ref[:, FE:] = jnp.zeros((SHARE, WIDE - FE), bf16)
+    out_ref[...] = mm_nt(order, act_ref[...]).astype(bf16)
+
+
+def lanes(rows):
+    return lax.broadcasted_iota(jnp.int32, (rows, 128), 1)
+
+
+def pack(block):
+    tail = block[:, TAIL:]
+    last = jnp.where(lanes(8) < 64, tail[:8], pltpu.roll(tail[8:], 64, 1))
+    return jnp.concatenate([block[:, at : at + 128] for at in range(0, TAIL, 128)] + [last], axis=0)
+
+
+def unpack_tail(last):
+    upper = jnp.where(lanes(8) < 64, last, 0.0)
+    lower = jnp.where(lanes(8) < 64, pltpu.roll(last, 64, 1), 0.0)
+    return jnp.concatenate([upper, lower], axis=0)
+
+
+def unpack(lines):
+    tiles = [lines[at // 8 : at // 8 + BLOCK] for at in range(0, TAIL, 128)]
+    return jnp.concatenate(tiles + [unpack_tail(lines[LINES - 8 :])], axis=1)
+
+
+def gradient_kernel(left_ref, cot_ref, out_ref, wide_ref):
+    wide_ref[:, :FE] = mm_nt(left_ref[...], cot_ref[...])
+    wide_ref[:, FE:] = jnp.zeros((SHARE, WIDE - FE), f32)
+    for m in range(SHARE // BLOCK):
+        out_ref[m] = pack(wide_ref[m * BLOCK : (m + 1) * BLOCK, :]).astype(bf16)
 
 
 def own_rows_mask():
@@ -72,7 +102,7 @@
 
 def share_kernel(near_ref, mom_ref, exact_ref, out_ref):
     partial = jnp.sum(near_ref[...].astype(f32), axis=0)
-    own = jnp.where(own_rows_mask(), place_rows(mom_ref), 0.0)
+    own = pack(jnp.where(own_rows_mask(), place_rows(mom_ref), 0.0))
     share = 1.95 * partial + (0.95 * 0.95) * own
     exact_ref[...] = share
     out_ref[...] = jnp.broadcast_to(share.astype(bf16)[None], out_ref.shape)
@@ -82,7 +112,7 @@
     total = jnp.sum(far_ref[...].astype(f32), axis=0)
     rows_ref[...] = jnp.broadcast_to(total.astype(bf16)[None], rows_ref.shape)
     exact = exact_ref[...]
-    better = total + (exact - exact.astype(bf16).astype(f32))
+    better = unpack(total + (exact - exact.astype(bf16).astype(f32)))
     mine = jnp.where(own_rows_mask(), better, 0.0)
     odd = (lax.broadcasted_iota(jnp.int32, (BLOCK, WIDE), 0) & 1) == 1
     own_ref[...] = jnp.zeros_like(own_ref)
@@ -97,7 +127,13 @@
         at += WIDE - first
 
 
-def gram_kernel(rows_ref, out_ref):
+def gram_kernel(packed_ref, out_ref, rows_ref):
+    for m in range(1024 // BLOCK):
+        rows = pl.ds(m * BLOCK, BLOCK)
+        for at in range(0, TAIL, 128):
+            rows_ref[rows, at : at + 128] = packed_ref[m, at // 8 : at // 8 + BLOCK, :]
+        last = packed_ref[m].astype(f32)[LINES - 8 :]
+        rows_ref[rows, TAIL:] = unpack_tail(last).astype(bf16)
     for first, at, width in packed_blocks():
         out_ref[:, at : at + width] = lax.dot_general(
             rows_ref[:, first : first + TILE],
@@ -182,18 +218,23 @@
 
 def per_device(activations, cotangent, momentum):
     momentum = momentum[0]
-    partial = kernel_call(gradient_kernel, shape((SHARE, WIDE), bf16), 2)(activations, cotangent.T)
-    near = exchange(partial.reshape(16, BLOCK, WIDE), NEAR)
+    left = kernel_call(order_kernel, shape((SHARE, 512), bf16), 1, cost=COST)(activations)
+    partial = kernel_call(
+        gradient_kernel, shape((16, LINES, 128), bf16), 2, [pltpu.VMEM((SHARE, WIDE), f32)]
+    )(left, cotangent.T)
+    near = exchange(partial, NEAR)
     exact, share = kernel_call(
-        share_kernel, (shape((BLOCK, WIDE), f32), shape((8, BLOCK, WIDE), bf16)), 2
+        share_kernel, (shape((LINES, 128), f32), shape((8, LINES, 128), bf16)), 2
     )(near, momentum)
     far = exchange(share, FAR)
     rows, own = kernel_call(
-        direction_kernel, (shape((4, BLOCK, WIDE), bf16), shape((16, WIDE), f32)), 2
+        direction_kernel, (shape((4, LINES, 128), bf16), shape((16, WIDE), f32)), 2
     )(far, exact)
-    rows = exchange(rows, OWNERS).reshape(64, WIDE)
-    rows = exchange(jnp.broadcast_to(rows[None], (16, 64, WIDE)), NEAR).reshape(1024, WIDE)
-    mine = kernel_call(gram_kernel, shape((TILE, 1536), bf16), 1)(rows)
+    rows = exchange(rows, OWNERS)
+    rows = exchange(jnp.broadcast_to(rows[None], (16, 4, LINES, 128)), NEAR)
+    mine = kernel_call(
+        gram_kernel, shape((TILE, 1536), bf16), 1, [pltpu.VMEM((1024, WIDE), bf16)]
+    )(rows.reshape(64, LINES, 128))
     other = lax.ppermute(mine, "core", [(0, 1), (1, 0)])
     gradient = (own[:2, :FE] - (0.95 * 0.95) * momentum) / 1.95
     momentum_new = 0.95 * momentum + gradient

time: 99.4 us -> 97 us (0.976)
  blocking collectives: 76.3 us -> 75.3 us
    unnamed x6, local copies, waits for them, and re-layouts: 2.06 us -> 1.02 us
    pallas_call x4 -> x5, Pallas kernels: 1.71 us -> 2.13 us  [the longest x1 1.12 us: per_device(): kernel_call(gram_kernel, shape((TILE, 1536), bf16), 1, [pltpu.VMEM((1024,...]
where the time goes in v6:
time: 97 us; the launch traced here: 96.7 us
  blocking collectives  75.3 us (78%)
  starting transfers between devices  10.2 us (11%)
  Pallas kernels  7.39 us (8%)
  waiting for transfers between devices  1.29 us (1%)
  local copies, waits for them, and re-layouts  1.21 us (1%)
    all_to_all x4, blocking collectives, exchange(): return lax.all_to_all(blocks, axes, 0, 0, tiled=True)  75.3 us
    ppermute x1, starting transfers between devices, per_device(): other = lax.ppermute(mine, 'core', [(0, 1), (1, 0)])  10.2 us
    pallas_call x1, Pallas kernels, per_device(): kernel_call(newton_schulz_kernel, shape((2, FE), bf16), 3, [pltpu.VMEM((W...  5.26 us
  transfers between devices with their start and end apart: 1, of which 1 were waited for; matrix products, arithmetic and copies ran while one was open for 1% of the time, Pallas kernels for 0%

profile of v6, /device:TPU:1, one launch (start us, length us, event | category | flops | bytes accessed | tf_op | source)
XLA Modules:
  0.0 96.7 jit_solution(18146329570204150622)
XLA Ops:
  0.6 0.0 copy-start
  0.6 0.0 copy-start.2
  0.6 1.0 %copy-done.2 = bf16[512,256]{1,0:T(8,128)(2,1)S(1)} copy-done((bf16[512,256]{1,0:T(8,128)(2,1)S(1)}, bf16[512,256]{1,0:T(8,128)(2,1)}, u32[]{:S(2)}) %copy-start.2) | copy-done | bytes 262168
  1.7 0.3 shard_map.50.left_ref
  1.9 0.0 copy-start.1
  1.9 0.0 copy-done
  2.0 0.5 shard_map.51
  2.5 14.2 %all_to_all.20.near_ref = bf16[16,88,128]{2,1,0:T(8,128)(2,1)S(1)} all-to-all(bf16[16,88,128]{2,1,0:T(8,128)(2,1)S(1)} %shard_map.51), channel_id=1, replica_groups=mesh['x'=4,'ylo'=2,'zhi'=8,'zlo'=2,'yhi'=4,'core'=2] {'x','ylo','zlo'}, dimensions={0} | all-to-all | bytes 720896 | tf_op jit(solution)/shard_map/all_to_all | solution.py:216
  16.6 0.0 copy-done.1
  16.6 0.1 shard_map.52
  16.8 32.0 %all_to_all.21.far_ref = bf16[8,88,128]{2,1,0:T(8,128)(2,1)S(1)} all-to-all(bf16[8,88,128]{2,1,0:T(8,128)(2,1)S(1)} %get-tuple-element.6), channel_id=1, replica_groups=mesh['x'=4,'ylo'=2,'zhi'=8,'zlo'=2,'yhi'=4,'core'=2] {'zhi'}, dimensions={0} | all-to-all | bytes 360448 | tf_op jit(solution)/shard_map/all_to_all | solution.py:216
  48.8 0.1 shard_map.53
  48.9 12.7 %all_to_all.22 = bf16[4,88,128]{2,1,0:T(8,128)(2,1)S(1)} all-to-all(bf16[4,88,128]{2,1,0:T(8,128)(2,1)S(1)} %get-tuple-element.8), channel_id=1, replica_groups=mesh['x'=4,'ylo'=2,'zhi'=8,'zlo'=2,'yhi'=4,'core'=2] {'yhi'}, dimensions={0} | all-to-all | bytes 180224 | tf_op jit(solution)/shard_map/all_to_all | solution.py:216
  61.6 0.2 broadcast_in_dim.12
  61.8 16.4 %all_to_all.23 = bf16[16,4,88,128]{3,2,1,0:T(8,128)(2,1)S(1)} all-to-all(bf16[16,4,88,128]{3,2,1,0:T(8,128)(2,1)S(1)} %broadcast_in_dim.12), channel_id=1, replica_groups=mesh['x'=4,'ylo'=2,'zhi'=8,'zlo'=2,'yhi'=4,'core'=2] {'x','ylo','zlo'}, dimensions={0} | all-to-all | bytes 2883584 | tf_op jit(solution)/shard_map/all_to_all | solution.py:216
  78.2 1.1 %shard_map.54.mine_ref = bf16[256,1536]{1,0:T(8,128)(2,1)S(1)} custom-call(bf16[64,88,128]{2,1,0:T(8,128)(2,1)S(1)} %bitcast.7), custom_call_target="tpu_custom_call" | custom-call | tf_op jit(solution)/shard_map/pallas_call | solution.py:235
  79.4 10.2 %collective-permute-start = (bf16[256,1536]{1,0:T(8,128)(2,1)S(1)}, bf16[256,1536]{1,0:T(8,128)(2,1)S(1)}, u32[]{:S(2)}, u32[]{:S(2)}) collective-permute-start(bf16[256,1536]{1,0:T(8,128)(2,1)S(1)} %shard_map.54.mine_ref), channel_id=1, source_target_pairs={{0,1},{1,0},{2,3},{3,2},{4,5},{5,4},{6,7},{7,6},{8,9},{9,8},{10,11... | collective-permute-start | bytes 2359304 | tf_op jit(solution)/shard_map/ppermute | solution.py:238
  89.6 0.6 add_bitcast_fusion
  90.2 1.3 %collective-permute-done.other_ref = bf16[256,1536]{1,0:T(8,128)(2,1)S(1)} collective-permute-done((bf16[256,1536]{1,0:T(8,128)(2,1)S(1)}, bf16[256,1536]{1,0:T(8,128)(2,1)S(1)}, u32[]{:S(2)}, u32[]{:S(2)}) %collective-permute-start) | collective-permute-done | bytes 786464 | tf_op jit(solution)/shard_map/ppermute | solution.py:238
  91.4 5.3 %shard_map.55 = bf16[2,704]{1,0:T(2,128)(2,1)} custom-call(bf16[256,1536]{1,0:T(8,128)(2,1)S(1)} %shard_map.54.mine_ref, bf16[256,1536]{1,0:T(8,128)(2,1)S(1)} %collective-permute-done.other_ref, f32[16,768]{1,0:T(8,128)S(1)} %get-tuple-element.9.rows_ref), custom_call_target="tpu_custom_call" | custom-call | tf_op jit(solution)/shard_map/pallas_call | solution.py:241
Async XLA Ops:
  0.6 1.3 %copy-start = (bf16[512,704]{0,1:T(8,128)(2,1)S(1)}, bf16[512,704]{0,1:T(8,128)(2,1)}, u32[]{:S(2)}) copy-start(bf16[512,704]{0,1:T(8,128)(2,1)} %param.4) | copy-start | bytes 2162692
  0.6 1.0 %copy-start.2 = (bf16[512,256]{1,0:T(8,128)(2,1)S(1)}, bf16[512,256]{1,0:T(8,128)(2,1)}, u32[]{:S(2)}) copy-start(bf16[512,256]{1,0:T(8,128)(2,1)} %act_ref.1) | copy-start | bytes 786436
  1.9 14.7 %copy-start.1 = (f32[1,2,704]{2,1,0:T(2,128)S(1)}, f32[1,2,704]{2,1,0:T(2,128)}, u32[]{:S(2)}) copy-start(f32[1,2,704]{2,1,0:T(2,128)} %param.5) | copy-start | bytes 16900
  79.4 12.1 %collective-permute-start = (bf16[256,1536]{1,0:T(8,128)(2,1)S(1)}, bf16[256,1536]{1,0:T(8,128)(2,1)S(1)}, u32[]{:S(2)}, u32[]{:S(2)}) collective-permute-start(bf16[256,1536]{1,0:T(8,128)(2,1)S(1)} %shard_map.54.mine_ref), channel_id=1, source_target_pairs={{0,1},{1,0},{2,3},{3,2},{4,5},{5,4},{6,7},{7,6},{8,9},{9,8},{10,11... | collective-permute-start | bytes 2359304 | tf_op jit(solution)/shard_map/ppermute | solution.py:238

commit v7 on v6

--- a/solution.py
+++ b/solution.py
@@ -25,6 +25,7 @@
 NEAR = ("x", "ylo", "zlo")
 FAR = "zhi"
 OWNERS = "yhi"
+FAR_ORDER = [[0, 4, 2, 6, 1, 5, 3, 7]]
 
 f32 = jnp.float32
 COST = pl.CostEstimate(flops=4_000_000_000, bytes_accessed=1_000_000, transcendentals=0)
@@ -115,9 +116,10 @@
     better = unpack(total + (exact - exact.astype(bf16).astype(f32)))
     mine = jnp.where(own_rows_mask(), better, 0.0)
     odd = (lax.broadcasted_iota(jnp.int32, (BLOCK, WIDE), 0) & 1) == 1
-    own_ref[...] = jnp.zeros_like(own_ref)
-    own_ref[0:1, :] = jnp.sum(jnp.where(odd, 0.0, mine), axis=0, keepdims=True)
-    own_ref[1:2, :] = jnp.sum(jnp.where(odd, mine, 0.0), axis=0, keepdims=True)
+    first = jnp.sum(jnp.where(odd, 0.0, mine), axis=0, keepdims=True)
+    second = jnp.sum(jnp.where(odd, mine, 0.0), axis=0, keepdims=True)
+    row = lax.broadcasted_iota(jnp.int32, (16, WIDE), 0)
+    own_ref[...] = jnp.where(row < 6, jnp.where((row & 1) == 0, first, second), 0.0)
 
 
 def packed_blocks():
@@ -195,17 +197,18 @@
     x = step(x).astype(bf16)
     one_side(left_ref, poly_ref, gram_ref, gram_ref)
     one_side(next_ref, left_ref, poly_ref, left_ref)
+    group = lax.broadcasted_iota(jnp.int32, (16, WIDE), 0) >> 1
+    stack = jnp.where(group == 0, x.astype(f32), mm(x, next_ref[...]))
+    stack = jnp.where(group == 2, mm(stack.astype(bf16), next_ref[...]), stack)
     polynomial(next_ref)
-    x = step(x).astype(bf16)
-
-    def last_gram(rows):
-        rows = step(rows).astype(bf16)
-        return step(mm(rows, next_ref[...]).astype(bf16))
-
-    once = last_gram(x)
-    twice = last_gram(once.astype(bf16))
-    x = (quintic_a * x.astype(f32) + (quintic_b * once + quintic_c * twice)).astype(bf16)
-    out_ref[...] = (step_scale * x.astype(f32)).astype(bf16)[:2, :FE]
+    powers = []
+    for _ in range(5):
+        stack = step(stack.astype(bf16))
+        powers.append(stack)
+    x = powers[0][:2].astype(bf16).astype(f32)
+    once, twice = powers[2][2:4], powers[4][4:6]
+    x = (quintic_a * x + (quintic_b * once + quintic_c * twice)).astype(bf16)
+    out_ref[...] = (step_scale * x.astype(f32)).astype(bf16)[:, :FE]
 
 
 def shape(dims, dtype):
@@ -226,7 +229,7 @@
     exact, share = kernel_call(
         share_kernel, (shape((LINES, 128), f32), shape((8, LINES, 128), bf16)), 2
     )(near, momentum)
-    far = exchange(share, FAR)
+    far = lax.all_to_all(share, FAR, 0, 0, axis_index_groups=FAR_ORDER, tiled=True)
     rows, own = kernel_call(
         direction_kernel, (shape((4, LINES, 128), bf16), shape((16, WIDE), f32)), 2
     )(far, exact)

time: 97 us -> 96.5 us (level)
    all_to_all x0 -> x1, blocking collectives: none -> 29.2 us  [per_device(): lax.all_to_all(share, FAR, 0, 0, axis_index_groups=FAR_ORDER, tiled=True)]
    all_to_all x4 -> x3, blocking collectives: 75.3 us -> 46.6 us  [exchange(): return lax.all_to_all(blocks, axes, 0, 0, tiled=True)]
where the time goes in v7:
time: 96.5 us; the launch traced here: 96.2 us
  blocking collectives  75.7 us (78%)
  starting transfers between devices  9.39 us (10%)
  Pallas kernels  7.33 us (8%)
  waiting for transfers between devices  1.29 us (1%)
  local copies, waits for them, and re-layouts  1.21 us (1%)
    all_to_all x3, blocking collectives, exchange(): return lax.all_to_all(blocks, axes, 0, 0, tiled=True)  46.6 us
    all_to_all x1, blocking collectives, per_device(): lax.all_to_all(share, FAR, 0, 0, axis_index_groups=FAR_ORDER, tiled=True)  29.2 us
    ppermute x1, starting transfers between devices, per_device(): other = lax.ppermute(mine, 'core', [(0, 1), (1, 0)])  9.39 us
    pallas_call x1, Pallas kernels, per_device(): kernel_call(newton_schulz_kernel, shape((2, FE), bf16), 3, [pltpu.VMEM((W...  5.2 us
  transfers between devices with their start and end apart: 1, of which 1 were waited for; matrix products, arithmetic and copies ran while one was open for 1% of the time, Pallas kernels for 0%

profile of v7, /device:TPU:1, one launch (start us, length us, event | category | flops | bytes accessed | tf_op | source)
XLA Modules:
  0.0 96.2 jit_solution(2699109111021301986)
XLA Ops:
  0.6 0.0 copy-start
  0.6 0.0 copy-start.2
  0.6 1.0 %copy-done.2 = bf16[512,256]{1,0:T(8,128)(2,1)S(1)} copy-done((bf16[512,256]{1,0:T(8,128)(2,1)S(1)}, bf16[512,256]{1,0:T(8,128)(2,1)}, u32[]{:S(2)}) %copy-start.2) | copy-done | bytes 262168
  1.7 0.3 shard_map.50.left_ref
  1.9 0.0 copy-start.1
  1.9 0.0 copy-done
  2.0 0.5 shard_map.51
  2.5 14.2 %all_to_all.20.near_ref = bf16[16,88,128]{2,1,0:T(8,128)(2,1)S(1)} all-to-all(bf16[16,88,128]{2,1,0:T(8,128)(2,1)S(1)} %shard_map.51), channel_id=1, replica_groups=mesh['x'=4,'ylo'=2,'zhi'=8,'zlo'=2,'yhi'=4,'core'=2] {'x','ylo','zlo'}, dimensions={0} | all-to-all | bytes 720896 | tf_op jit(solution)/shard_map/all_to_all | solution.py:219
  16.6 0.0 copy-done.1
  16.6 0.1 shard_map.52
  16.8 29.2 %all_to_all.21.far_ref = bf16[8,88,128]{2,1,0:T(8,128)(2,1)S(1)} all-to-all(bf16[8,88,128]{2,1,0:T(8,128)(2,1)S(1)} %get-tuple-element.6), channel_id=1, replica_groups={{0,64,32,96,16,80,48,112},{1,65,33,97,17,81,49,113},{2,66,34,98,18,82,5..., dimensions={0} | all-to-all | bytes 360448 | tf_op jit(solution)/shard_map/all_to_all | solution.py:232
  45.9 0.1 shard_map.53
  46.0 12.8 %all_to_all.22 = bf16[4,88,128]{2,1,0:T(8,128)(2,1)S(1)} all-to-all(bf16[4,88,128]{2,1,0:T(8,128)(2,1)S(1)} %get-tuple-element.8), channel_id=1, replica_groups=mesh['x'=4,'ylo'=2,'zhi'=8,'zlo'=2,'yhi'=4,'core'=2] {'yhi'}, dimensions={0} | all-to-all | bytes 180224 | tf_op jit(solution)/shard_map/all_to_all | solution.py:219
  58.9 0.2 broadcast_in_dim.12
  59.0 19.6 %all_to_all.23 = bf16[16,4,88,128]{3,2,1,0:T(8,128)(2,1)S(1)} all-to-all(bf16[16,4,88,128]{3,2,1,0:T(8,128)(2,1)S(1)} %broadcast_in_dim.12), channel_id=1, replica_groups=mesh['x'=4,'ylo'=2,'zhi'=8,'zlo'=2,'yhi'=4,'core'=2] {'x','ylo','zlo'}, dimensions={0} | all-to-all | bytes 2883584 | tf_op jit(solution)/shard_map/all_to_all | solution.py:219
  78.6 1.1 %shard_map.54.mine_ref = bf16[256,1536]{1,0:T(8,128)(2,1)S(1)} custom-call(bf16[64,88,128]{2,1,0:T(8,128)(2,1)S(1)} %bitcast.7), custom_call_target="tpu_custom_call" | custom-call | tf_op jit(solution)/shard_map/pallas_call | solution.py:238
  79.7 9.4 %collective-permute-start = (bf16[256,1536]{1,0:T(8,128)(2,1)S(1)}, bf16[256,1536]{1,0:T(8,128)(2,1)S(1)}, u32[]{:S(2)}, u32[]{:S(2)}) collective-permute-start(bf16[256,1536]{1,0:T(8,128)(2,1)S(1)} %shard_map.54.mine_ref), channel_id=1, source_target_pairs={{0,1},{1,0},{2,3},{3,2},{4,5},{5,4},{6,7},{7,6},{8,9},{9,8},{10,11... | collective-permute-start | bytes 2359304 | tf_op jit(solution)/shard_map/ppermute | solution.py:241
  89.1 0.6 add_bitcast_fusion
  89.7 1.3 %collective-permute-done.other_ref = bf16[256,1536]{1,0:T(8,128)(2,1)S(1)} collective-permute-done((bf16[256,1536]{1,0:T(8,128)(2,1)S(1)}, bf16[256,1536]{1,0:T(8,128)(2,1)S(1)}, u32[]{:S(2)}, u32[]{:S(2)}) %collective-permute-start) | collective-permute-done | bytes 786464 | tf_op jit(solution)/shard_map/ppermute | solution.py:241
  91.0 5.2 %shard_map.55 = bf16[2,704]{1,0:T(2,128)(2,1)} custom-call(bf16[256,1536]{1,0:T(8,128)(2,1)S(1)} %shard_map.54.mine_ref, bf16[256,1536]{1,0:T(8,128)(2,1)S(1)} %collective-permute-done.other_ref, f32[16,768]{1,0:T(8,128)S(1)} %get-tuple-element.9.rows_ref), custom_call_target="tpu_custom_call" | custom-call | tf_op jit(solution)/shard_map/pallas_call | solution.py:244
Async XLA Ops:
  0.6 1.3 %copy-start = (bf16[512,704]{0,1:T(8,128)(2,1)S(1)}, bf16[512,704]{0,1:T(8,128)(2,1)}, u32[]{:S(2)}) copy-start(bf16[512,704]{0,1:T(8,128)(2,1)} %param.4) | copy-start | bytes 2162692
  0.6 1.0 %copy-start.2 = (bf16[512,256]{1,0:T(8,128)(2,1)S(1)}, bf16[512,256]{1,0:T(8,128)(2,1)}, u32[]{:S(2)}) copy-start(bf16[512,256]{1,0:T(8,128)(2,1)} %act_ref.1) | copy-start | bytes 786436
  1.9 14.7 %copy-start.1 = (f32[1,2,704]{2,1,0:T(2,128)S(1)}, f32[1,2,704]{2,1,0:T(2,128)}, u32[]{:S(2)}) copy-start(f32[1,2,704]{2,1,0:T(2,128)} %param.5) | copy-start | bytes 16900
  79.7 11.3 %collective-permute-start = (bf16[256,1536]{1,0:T(8,128)(2,1)S(1)}, bf16[256,1536]{1,0:T(8,128)(2,1)S(1)}, u32[]{:S(2)}, u32[]{:S(2)}) collective-permute-start(bf16[256,1536]{1,0:T(8,128)(2,1)S(1)} %shard_map.54.mine_ref), channel_id=1, source_target_pairs={{0,1},{1,0},{2,3},{3,2},{4,5},{5,4},{6,7},{7,6},{8,9},{9,8},{10,11... | collective-permute-start | bytes 2359304 | tf_op jit(solution)/shard_map/ppermute | solution.py:241

commit v8 on v6

--- a/solution.py
+++ b/solution.py
@@ -24,7 +24,9 @@
 SIZES = (4, 2, 8, 2, 4, 2)
 NEAR = ("x", "ylo", "zlo")
 FAR = "zhi"
-OWNERS = "yhi"
+FAR_ORDER = [[0, 4, 2, 6, 1, 5, 3, 7]]
+OWNERS = ('ylo', 'yhi')
+LAST = ('x', 'zlo')
 
 f32 = jnp.float32
 COST = pl.CostEstimate(flops=4_000_000_000, bytes_accessed=1_000_000, transcendentals=0)
@@ -226,12 +228,12 @@
     exact, share = kernel_call(
         share_kernel, (shape((LINES, 128), f32), shape((8, LINES, 128), bf16)), 2
     )(near, momentum)
-    far = exchange(share, FAR)
+    far = lax.all_to_all(share, FAR, 0, 0, axis_index_groups=FAR_ORDER, tiled=True)
     rows, own = kernel_call(
-        direction_kernel, (shape((4, LINES, 128), bf16), shape((16, WIDE), f32)), 2
+        direction_kernel, (shape((8, LINES, 128), bf16), shape((16, WIDE), f32)), 2
     )(far, exact)
     rows = exchange(rows, OWNERS)
-    rows = exchange(jnp.broadcast_to(rows[None], (16, 4, LINES, 128)), NEAR)
+    rows = exchange(jnp.broadcast_to(rows[None], (8, 8, LINES, 128)), LAST)
     mine = kernel_call(
         gram_kernel, shape((TILE, 1536), bf16), 1, [pltpu.VMEM((1024, WIDE), bf16)]
     )(rows.reshape(64, LINES, 128))

time: 97 us -> 96 us (0.990)
  starting transfers between devices: 10.2 us -> 7.82 us
  blocking collectives: 75.3 us -> 76.7 us
    all_to_all x0 -> x1, blocking collectives: none -> 29.2 us  [per_device(): lax.all_to_all(share, FAR, 0, 0, axis_index_groups=FAR_ORDER, tiled=True)]
    all_to_all x4 -> x3, blocking collectives: 75.3 us -> 47.6 us  [exchange(): return lax.all_to_all(blocks, axes, 0, 0, tiled=True)]
    ppermute x1, starting transfers between devices: 10.2 us -> 7.82 us  [per_device(): other = lax.ppermute(mine, 'core', [(0, 1), (1, 0)])]
where the time goes in v8:
time: 96 us; the launch traced here: 95.7 us
  blocking collectives  76.7 us (80%)
  starting transfers between devices  7.82 us (8%)
  Pallas kernels  7.4 us (8%)
  waiting for transfers between devices  1.29 us (1%)
  local copies, waits for them, and re-layouts  1.21 us (1%)
    all_to_all x3, blocking collectives, exchange(): return lax.all_to_all(blocks, axes, 0, 0, tiled=True)  47.6 us
    all_to_all x1, blocking collectives, per_device(): lax.all_to_all(share, FAR, 0, 0, axis_index_groups=FAR_ORDER, tiled=True)  29.2 us
    ppermute x1, starting transfers between devices, per_device(): other = lax.ppermute(mine, 'core', [(0, 1), (1, 0)])  7.82 us
    pallas_call x1, Pallas kernels, per_device(): kernel_call(newton_schulz_kernel, shape((2, FE), bf16), 3, [pltpu.VMEM((W...  5.26 us
  transfers between devices with their start and end apart: 1, of which 1 were waited for; matrix products, arithmetic and copies ran while one was open for 1% of the time, Pallas kernels for 0%

profile of v8, /device:TPU:1, one launch (start us, length us, event | category | flops | bytes accessed | tf_op | source)
XLA Modules:
  0.0 95.7 jit_solution(7145526757890650609)
XLA Ops:
  0.6 0.0 copy-start
  0.6 0.0 copy-start.2
  0.6 1.0 %copy-done.2 = bf16[512,256]{1,0:T(8,128)(2,1)S(1)} copy-done((bf16[512,256]{1,0:T(8,128)(2,1)S(1)}, bf16[512,256]{1,0:T(8,128)(2,1)}, u32[]{:S(2)}) %copy-start.2) | copy-done | bytes 262168
  1.7 0.3 shard_map.50.left_ref
  1.9 0.0 copy-start.1
  1.9 0.0 copy-done
  2.0 0.5 shard_map.51
  2.5 14.2 %all_to_all.20.near_ref = bf16[16,88,128]{2,1,0:T(8,128)(2,1)S(1)} all-to-all(bf16[16,88,128]{2,1,0:T(8,128)(2,1)S(1)} %shard_map.51), channel_id=1, replica_groups=mesh['x'=4,'ylo'=2,'zhi'=8,'zlo'=2,'yhi'=4,'core'=2] {'x','ylo','zlo'}, dimensions={0} | all-to-all | bytes 720896 | tf_op jit(solution)/shard_map/all_to_all | solution.py:218
  16.6 0.0 copy-done.1
  16.6 0.1 shard_map.52
  16.8 29.2 %all_to_all.21.far_ref = bf16[8,88,128]{2,1,0:T(8,128)(2,1)S(1)} all-to-all(bf16[8,88,128]{2,1,0:T(8,128)(2,1)S(1)} %get-tuple-element.6), channel_id=1, replica_groups={{0,64,32,96,16,80,48,112},{1,65,33,97,17,81,49,113},{2,66,34,98,18,82,5..., dimensions={0} | all-to-all | bytes 360448 | tf_op jit(solution)/shard_map/all_to_all | solution.py:231
  45.9 0.1 shard_map.53
  46.0 12.9 %all_to_all.22 = bf16[8,88,128]{2,1,0:T(8,128)(2,1)S(1)} all-to-all(bf16[8,88,128]{2,1,0:T(8,128)(2,1)S(1)} %get-tuple-element.8), channel_id=1, replica_groups=mesh['x'=4,'ylo'=2,'zhi'=8,'zlo'=2,'yhi'=4,'core'=2] {'ylo','yhi'}, dimensions={0} | all-to-all | bytes 360448 | tf_op jit(solution)/shard_map/all_to_all | solution.py:218
  59.0 0.2 broadcast_in_dim.12
  59.2 20.5 %all_to_all.23 = bf16[8,8,88,128]{3,2,1,0:T(8,128)(2,1)S(1)} all-to-all(bf16[8,8,88,128]{3,2,1,0:T(8,128)(2,1)S(1)} %broadcast_in_dim.12), channel_id=1, replica_groups=mesh['x'=4,'ylo'=2,'zhi'=8,'zlo'=2,'yhi'=4,'core'=2] {'x','zlo'}, dimensions={0} | all-to-all | bytes 2883584 | tf_op jit(solution)/shard_map/all_to_all | solution.py:218
  79.6 1.1 %shard_map.54.mine_ref = bf16[256,1536]{1,0:T(8,128)(2,1)S(1)} custom-call(bf16[64,88,128]{2,1,0:T(8,128)(2,1)S(1)} %bitcast.7), custom_call_target="tpu_custom_call" | custom-call | tf_op jit(solution)/shard_map/pallas_call | solution.py:237
  80.7 7.8 %collective-permute-start = (bf16[256,1536]{1,0:T(8,128)(2,1)S(1)}, bf16[256,1536]{1,0:T(8,128)(2,1)S(1)}, u32[]{:S(2)}, u32[]{:S(2)}) collective-permute-start(bf16[256,1536]{1,0:T(8,128)(2,1)S(1)} %shard_map.54.mine_ref), channel_id=1, source_target_pairs={{0,1},{1,0},{2,3},{3,2},{4,5},{5,4},{6,7},{7,6},{8,9},{9,8},{10,11... | collective-permute-start | bytes 2359304 | tf_op jit(solution)/shard_map/ppermute | solution.py:240
  88.6 0.6 add_bitcast_fusion
  89.2 1.3 %collective-permute-done.other_ref = bf16[256,1536]{1,0:T(8,128)(2,1)S(1)} collective-permute-done((bf16[256,1536]{1,0:T(8,128)(2,1)S(1)}, bf16[256,1536]{1,0:T(8,128)(2,1)S(1)}, u32[]{:S(2)}, u32[]{:S(2)}) %collective-permute-start) | collective-permute-done | bytes 786464 | tf_op jit(solution)/shard_map/ppermute | solution.py:240
  90.5 5.3 %shard_map.55 = bf16[2,704]{1,0:T(2,128)(2,1)} custom-call(bf16[256,1536]{1,0:T(8,128)(2,1)S(1)} %shard_map.54.mine_ref, bf16[256,1536]{1,0:T(8,128)(2,1)S(1)} %collective-permute-done.other_ref, f32[16,768]{1,0:T(8,128)S(1)} %get-tuple-element.9.rows_ref), custom_call_target="tpu_custom_call" | custom-call | tf_op jit(solution)/shard_map/pallas_call | solution.py:243
Async XLA Ops:
  0.6 1.3 %copy-start = (bf16[512,704]{0,1:T(8,128)(2,1)S(1)}, bf16[512,704]{0,1:T(8,128)(2,1)}, u32[]{:S(2)}) copy-start(bf16[512,704]{0,1:T(8,128)(2,1)} %param.4) | copy-start | bytes 2162692
  0.6 1.0 %copy-start.2 = (bf16[512,256]{1,0:T(8,128)(2,1)S(1)}, bf16[512,256]{1,0:T(8,128)(2,1)}, u32[]{:S(2)}) copy-start(bf16[512,256]{1,0:T(8,128)(2,1)} %act_ref.1) | copy-start | bytes 786436
  1.9 14.7 %copy-start.1 = (f32[1,2,704]{2,1,0:T(2,128)S(1)}, f32[1,2,704]{2,1,0:T(2,128)}, u32[]{:S(2)}) copy-start(f32[1,2,704]{2,1,0:T(2,128)} %param.5) | copy-start | bytes 16900
  80.7 9.7 %collective-permute-start = (bf16[256,1536]{1,0:T(8,128)(2,1)S(1)}, bf16[256,1536]{1,0:T(8,128)(2,1)S(1)}, u32[]{:S(2)}, u32[]{:S(2)}) collective-permute-start(bf16[256,1536]{1,0:T(8,128)(2,1)S(1)} %shard_map.54.mine_ref), channel_id=1, source_target_pairs={{0,1},{1,0},{2,3},{3,2},{4,5},{5,4},{6,7},{7,6},{8,9},{9,8},{10,11... | collective-permute-start | bytes 2359304 | tf_op jit(solution)/shard_map/ppermute | solution.py:240
